TPU v7x, 512 devices: a whole 4x4x16 slice. The times are simulated.
512 devices in a mesh: facet: 64 (over z, y), pol: 4 (over x), tm: 2 (over core).
Axes of the slice: x: 4, y: 4, z: 16, core: 2. Of those that a mesh axis runs over, the one named last changes fastest.
Arguments:
- tile_spectral_lines: bfloat16 [64, 4, 2, 64, 4096], P('facet', 'pol', None, 'tm'), may hold values from -6 to 6
- taper_leading_axis: bfloat16 [64, 2, 128, 512], P('facet', 'tm'), may hold values from -0.25 to 0.25
- taper_trailing_axis: bfloat16 [64, 2, 128, 512], P('facet', 'tm'), may hold values from -0.25 to 0.25
- depth_layer_factors: bfloat16 [64, 2, 2, 128], P('facet', 'tm'), may hold values from -4 to 4
- measured_correlations: float32 [64, 8, 2, 128], P('facet', None, 'tm', 'pol'), may hold values from -6 to 6
- visibility_groups_table: int32 [64, 2, 3, 8], P('facet', 'tm'), may hold values from 0 to 130815, as said below
- antenna_links: int32 [2, 130816], replicated, may hold values from 0 to 511, as said below
- complex_receiver_factors: float32 [256, 4, 512], replicated, may hold values from -5 to 5
Outputs:
- residual: float32 [64, 8, 2, 128], P('facet', None, 'tm', 'pol')
- gain_grad: float32 [512, 1024], P(('facet', 'pol', 'tm'))
Inputs may be any that keep to these rules, and one draw needn't show every extreme that they name: `visibility_groups_table`: for each subgrid and owner, every block has a channel below 256, a count of 1 or more, and baselines offset to offset + count - 1 below 130816; the counts of one owner sum to at most 128, and some owner reaches 128 in every draw. `antenna_links`: each baseline joins two different stations.
All inputs are finite; a program needn't handle non-finite values.
Results may differ from a plain program's by a relative error of at most 0.012.
Values may be sent and summed in bfloat16 or wider, within the bound.
No kernel may reach another device: no remote copies, remote signals or barrier semaphores. Data moves between devices by JAX's collectives and lax.ppermute only.
A program may use at most 192 MiB of HBM per device.

v0:
```python
import math

import jax
import jax.numpy as jnp
import numpy as np
from jax import lax
from jax.sharding import PartitionSpec as P

FGRID = 8
FS = 4096
MC = 64
SG = 512
NPOL = 4
NW = 2
NCH = 256
NST = 512


w_chirp = 0.37
grad_scale = 0.1
feed_first = np.array([0, 0, 1, 1])
feed_second = np.array([0, 1, 0, 1])


def laid_out(blocks, dim):
    blocks = jnp.moveaxis(blocks, 0, dim)
    lengths = blocks.shape
    return blocks.reshape(*lengths[:dim], lengths[dim] * lengths[dim + 1], *lengths[dim + 2 :])


def from_everyone(shard, axis):
    copies = jnp.broadcast_to(shard, (lax.axis_size(axis), *shard.shape))
    return lax.all_to_all(copies, axis, split_axis=0, concat_axis=0, tiled=True)


def collect(shard, axis, dim):
    return laid_out(from_everyone(shard, axis), dim)


def dft_table(length):
    indices = jnp.arange(length, dtype=jnp.int32)
    product = indices[:, None] * indices[None, :] % length
    angles = 2.0 * math.pi / length * product.astype(jnp.float32)
    factor = 1.0 / math.sqrt(length)
    return (
        (jnp.cos(angles) * factor).astype(jnp.bfloat16),
        (jnp.sin(angles) * factor).astype(jnp.bfloat16),
    )


def phase_table(left_size, right_size, length):
    left_index = jnp.arange(left_size, dtype=jnp.int32)
    right_index = jnp.arange(right_size, dtype=jnp.int32)
    product = left_index[:, None] * right_index[None, :] % length
    angles = 2.0 * math.pi / length * product.astype(jnp.float32)
    return (jnp.cos(angles), -jnp.sin(angles))


def chirp_phase(row_total, side_cells):
    across = (jnp.arange(row_total, dtype=jnp.int32) - side_cells // 2).astype(jnp.float32)
    downward = (jnp.arange(side_cells, dtype=jnp.int32) - side_cells // 2).astype(jnp.float32)
    return (
        w_chirp
        * (across[:, None] * across[:, None] + downward[None, :] * downward[None, :])
        / float(side_cells * side_cells)
    )


def make_planes(sub_real, sub_imag, phase_grid, layers):
    planes_list = []
    for plane_index in range(layers):
        angles = 2.0 * math.pi * plane_index * phase_grid
        cosine = jnp.cos(angles)
        sine_part = jnp.sin(angles)
        planes_list.append(
            jnp.stack(
                [sub_real * cosine - sub_imag * sine_part, sub_real * sine_part + sub_imag * cosine]
            ).astype(jnp.bfloat16)
        )
    return jnp.stack(planes_list)


def decode_slots(block_table, slot_index):
    channels = block_table[..., 0, :]
    offsets = block_table[..., 1, :]
    amounts = block_table[..., 2, :]
    starts = jnp.cumsum(amounts, axis=-1) - amounts
    relative = slot_index[:, None] - starts[..., None, :]
    member = ((relative >= 0) & (relative < amounts[..., None, :])).astype(jnp.int32)
    slot_live = jnp.sum(member, axis=-1)
    channel = jnp.sum(member * channels[..., None, :], axis=-1)
    antenna_couple = jnp.sum(member * (offsets[..., None, :] + relative), axis=-1)
    return (slot_live, channel, antenna_couple)


def model_terms(pred_re, pred_im, obs_re, obs_im, gain_first, gain_second, slot_live):
    first_re = gain_first[..., 2 * feed_first]
    first_im = gain_first[..., 2 * feed_first + 1]
    second_re = gain_second[..., 2 * feed_second]
    second_im = gain_second[..., 2 * feed_second + 1]
    both_re = first_re * second_re + first_im * second_im
    both_im = first_im * second_re - first_re * second_im
    model_re = both_re * pred_re - both_im * pred_im
    model_im = both_re * pred_im + both_im * pred_re
    alive_mask = slot_live.astype(jnp.float32)[..., None]
    resid_re = alive_mask * (obs_re - model_re)
    resid_im = alive_mask * (obs_im - model_im)
    cross_re = second_re * pred_re + second_im * pred_im
    cross_im = second_im * pred_re - second_re * pred_im
    lead_re = -(resid_re * cross_re - resid_im * cross_im)
    lead_im = -(resid_re * cross_im + resid_im * cross_re)
    along_re = first_re * pred_re - first_im * pred_im
    along_im = first_re * pred_im + first_im * pred_re
    trail_re = -(resid_re * along_re + resid_im * along_im)
    trail_im = -(resid_re * along_im - resid_im * along_re)
    leading = jnp.stack(
        [
            lead_re[..., 0] + lead_re[..., 1],
            lead_im[..., 0] + lead_im[..., 1],
            lead_re[..., 2] + lead_re[..., 3],
            lead_im[..., 2] + lead_im[..., 3],
        ],
        axis=-1,
    )
    trailing = jnp.stack(
        [
            trail_re[..., 0] + trail_re[..., 2],
            trail_im[..., 0] + trail_im[..., 2],
            trail_re[..., 1] + trail_re[..., 3],
            trail_im[..., 1] + trail_im[..., 3],
        ],
        axis=-1,
    )
    return (resid_re, resid_im, leading, trailing)


def degrid_block(layers, rows_u, rows_v, weights_w):
    spread_v = jnp.einsum("wcuv,nv->wcun", layers, rows_v, preferred_element_type=jnp.float32)
    along_u = jnp.sum(spread_v * jnp.transpose(rows_u).astype(jnp.float32)[None, None], axis=2)
    return jnp.sum(along_u * weights_w.astype(jnp.float32)[:, None, :], axis=0)


def on_device(
    tile_spectral_lines,
    taper_leading_axis,
    taper_trailing_axis,
    depth_layer_factors,
    measured_correlations,
    visibility_groups_table,
    antenna_links,
    complex_receiver_factors,
):
    careful = lax.Precision.HIGH
    facet_total = tile_spectral_lines.shape[0]
    row_share = tile_spectral_lines.shape[3]
    spread = FS // MC
    subgrids = lax.axis_size("facet")
    source = (
        tile_spectral_lines[:, 0].astype(jnp.float32).reshape(facet_total, 2, row_share, MC, spread)
    )
    source_re = source[:, 0]
    source_im = source[:, 1]
    inner_re, inner_im = phase_table(MC, MC, MC)
    section_re = jnp.einsum("fmar,ak->fmkr", source_re, inner_re, precision=careful) - jnp.einsum(
        "fmar,ak->fmkr", source_im, inner_im, precision=careful
    )
    section_im = jnp.einsum("fmar,ak->fmkr", source_re, inner_im, precision=careful) + jnp.einsum(
        "fmar,ak->fmkr", source_im, inner_re, precision=careful
    )
    twist_re, twist_im = phase_table(MC, spread, FS)
    turned_re = section_re * twist_re - section_im * twist_im
    turned_im = section_re * twist_im + section_im * twist_re
    outer_re, outer_im = phase_table(spread, subgrids, spread)
    factor = 1.0 / math.sqrt(FS)
    contrib_re = (
        jnp.einsum("fmkr,rs->sfmk", turned_re, outer_re, precision=careful)
        - jnp.einsum("fmkr,rs->sfmk", turned_im, outer_im, precision=careful)
    ) * factor
    contrib_im = (
        jnp.einsum("fmkr,rs->sfmk", turned_re, outer_im, precision=careful)
        + jnp.einsum("fmkr,rs->sfmk", turned_im, outer_re, precision=careful)
    ) * factor
    contrib = jnp.concatenate([contrib_re, contrib_im], axis=-1).astype(jnp.bfloat16)
    table_re, table_im = dft_table(SG)
    upper_half = jnp.concatenate([table_re, table_im], axis=1).reshape(FGRID, MC, 2 * SG)
    lower_half = jnp.concatenate([-table_im, table_re], axis=1).reshape(FGRID, MC, 2 * SG)
    stacked_table = jnp.stack([upper_half, lower_half], axis=1).reshape(FGRID, 2 * MC, 2 * SG)
    received = lax.all_to_all(contrib, "facet", split_axis=0, concat_axis=1, tiled=True)
    pieces = received.reshape(FGRID, FGRID, received.shape[2], 2 * MC)
    product = jnp.einsum("ijmc,jcv->imv", pieces, stacked_table, preferred_element_type=jnp.float32)
    half_rows = product.astype(jnp.bfloat16)
    whole_rows = collect(half_rows, "tm", 1).reshape(SG, 2 * SG)
    owners = lax.axis_size("tm")
    owner_index = lax.axis_index("tm")
    row_count = SG // owners
    slots_own = taper_leading_axis.shape[2]
    flat_u = taper_leading_axis.reshape(slots_own, SG)
    flat_v = taper_trailing_axis.reshape(slots_own, SG)
    flat_w = depth_layer_factors.reshape(NW, slots_own)
    first_row = owner_index * row_count
    part_re = lax.dynamic_slice_in_dim(table_re, first_row, row_count, 0)
    part_im = lax.dynamic_slice_in_dim(table_im, first_row, row_count, 0)
    upper_rows = jnp.dot(part_re, whole_rows, preferred_element_type=jnp.float32)
    lower_rows = jnp.dot(part_im, whole_rows, preferred_element_type=jnp.float32)
    sub_real = upper_rows[:, :SG] - lower_rows[:, SG:]
    sub_imag = upper_rows[:, SG:] + lower_rows[:, :SG]
    own_part = jnp.stack([sub_real, sub_imag]).astype(jnp.bfloat16)
    subgrid = collect(own_part, "tm", 1)
    layers = make_planes(subgrid[0], subgrid[1], chirp_phase(SG, SG), NW)
    predicted = degrid_block(layers, flat_u, flat_v, flat_w)
    regrouped = lax.all_to_all(predicted[None], "pol", split_axis=2, concat_axis=0, tiled=True)
    quarter = regrouped.shape[2]
    slot_index = lax.axis_index("pol") * quarter + jnp.arange(quarter, dtype=jnp.int32)
    slot_live, channel, antenna_couple = decode_slots(
        visibility_groups_table.reshape(3, visibility_groups_table.shape[3]), slot_index
    )
    antenna_left = jnp.take(antenna_links[0], antenna_couple)
    antenna_right = jnp.take(antenna_links[1], antenna_couple)
    gains_turned = jnp.transpose(complex_receiver_factors, (0, 2, 1))
    gain_first = gains_turned[channel, antenna_left]
    gain_second = gains_turned[channel, antenna_right]
    pred_re = jnp.transpose(regrouped[:, 0])
    pred_im = jnp.transpose(regrouped[:, 1])
    observed_local = measured_correlations.reshape(NPOL, 2, quarter)
    obs_re = jnp.transpose(observed_local[:, 0])
    obs_im = jnp.transpose(observed_local[:, 1])
    resid_re, resid_im, leading, trailing = model_terms(
        pred_re, pred_im, obs_re, obs_im, gain_first, gain_second, slot_live
    )
    residual = jnp.stack([jnp.transpose(resid_re), jnp.transpose(resid_im)], axis=1).reshape(
        1, 2 * NPOL, 1, quarter
    )
    channel_ids = jnp.arange(NCH, dtype=jnp.int32)
    own_count = NST // lax.axis_size(("facet", "pol", "tm"))
    own_stations = (
        lax.axis_index(("facet", "pol", "tm")) * own_count + jnp.arange(own_count, dtype=jnp.int32)
    ).astype(jnp.float32)
    channel_float = channel_ids.astype(jnp.float32)
    ident_rows = jnp.stack([antenna_left, antenna_right, channel]).astype(jnp.float32)
    records = jnp.concatenate([ident_rows, jnp.transpose(leading), jnp.transpose(trailing)], axis=0)
    piece = lax.all_gather(records, ("facet", "pol", "tm"), axis=1, tiled=True)
    piece_rows = piece.shape[1]
    group = math.gcd(piece_rows, 8 * quarter)
    grouped = jnp.transpose(piece.reshape(11, piece_rows // group, group), (1, 0, 2))

    def one_group(carry, record_block):
        match_first = (record_block[0][:, None] == own_stations[None, :]).astype(jnp.float32)
        match_second = (record_block[1][:, None] == own_stations[None, :]).astype(jnp.float32)
        weighted = (
            match_first[:, :, None] * jnp.transpose(record_block[3:7])[:, None, :]
            + match_second[:, :, None] * jnp.transpose(record_block[7:11])[:, None, :]
        )
        onehot = (record_block[2][:, None] == channel_float[None, :]).astype(jnp.float32)
        added = jnp.dot(
            jnp.transpose(weighted.reshape(group, own_count * 4)), onehot, precision=careful
        )
        return (carry + added.reshape(own_count, 4, NCH), None)

    result, unused = lax.scan(one_group, jnp.zeros((own_count, 4, NCH), jnp.float32), grouped)
    gain_grad = grad_scale * jnp.transpose(result, (0, 2, 1)).reshape(own_count, 4 * NCH)
    return (residual, gain_grad)


def solution(mesh):
    return jax.shard_map(
        on_device,
        mesh=mesh,
        in_specs=(
            P("facet", "pol", None, "tm", None),
            P("facet", "tm", None, None),
            P("facet", "tm", None, None),
            P("facet", "tm", None, None),
            P("facet", None, "tm", "pol"),
            P("facet", "tm", None, None),
            P(),
            P(),
        ),
        out_specs=(P("facet", None, "tm", "pol"), P(("facet", "pol", "tm"), None)),
        check_vma=False,
    )
```

profile of v0, /device:TPU:1, one launch (start us, length us, event | category | flops | bytes accessed | tf_op | source)
XLA Modules:
  0.0 288.1 jit_solution(2135503734819156724)
XLA Ops:
  0.6 2.1 reshape.857
  5.4 1.7 fusion.60
  7.1 1.7 fusion.58
  8.8 1.7 fusion.38
  10.5 1.7 fusion.37
  12.6 1.1 copy.72
  13.7 19.7 %all-to-all-start = ((bf16[64,1,32,128]{3,2,1,0:T(8,128)(2,1)}), bf16[64,1,32,128]{3,2,1,0:T(8,128)(2,1)}, u32[]{:S(2)}, u32[]{:S(2)}) async-start(bf16[64,1,32,128]{3,2,1,0:T(8,128)(2,1)} %copy.72), calls=%async_computation | async-start | bytes 1048576 | tf_op jit(solution)/shard_map/all_to_all | solution.py:188
  34.4 4.2 %slice_reduce_fusion.1 = (s32[130816]{0:T(1024)S(1)}, s32[130816]{0:T(1024)S(1)}) fusion(s32[2,130816]{1,0:T(2,128)} %param.26), kind=kLoop, calls=%fused_computation.123 | loop fusion | bytes 2093056 | tf_op jit(solution)/shard_map/slice | solution.py:217
  38.6 0.7 gather_fusion.6
  39.3 0.7 gather_fusion.7
  41.5 29.9 %copy.65 = f32[256,4,512]{1,2,0:T(8,128)} copy(f32[256,4,512]{2,1,0:T(4,128)S(1)} %copy-done.1) | data formatting | bytes 4194304 | tf_op args[7]
  71.4 1.4 gather_fusion
  74.0 1.9 gather_fusion.2
  78.3 4.3 %fusion.83 = bf16[8,1,64,512]{3,2,1,0:T(8,128)(2,1)S(1)} fusion(s32[8,64]{1,0:T(8,128)S(1)} %multiply_add_fusion.3), kind=kLoop, calls=%fused_computation.133 | loop fusion | flops 4980736 | bytes 526336 | tf_op jit(solution)/shard_map/neg | solution.py:186
  82.6 4.9 %multiply_convert_fusion = (bf16[8,1,64,512]{3,2,1,0:T(8,128)(2,1)S(1)}, bf16[8,1,64,512]{3,2,1,0:T(8,128)(2,1)S(1)}) fusion(s32[8,64]{1,0:T(8,128)S(1)} %multiply_add_fusion.3), kind=kLoop, calls=%fused_computation.96 | loop fusion | flops 4718592 | bytes 1050624 | tf_op jit(solution)/shard_map/convert_element_type | solution.py:47
  89.3 1.8 fusion.36
  91.2 5.1 %all_to_all.37 = bf16[2,8,32,1024]{3,2,1,0:T(8,128)(2,1)S(1)} all-to-all(bf16[2,8,32,1024]{3,2,1,0:T(8,128)(2,1)S(1)} %broadcast_in_dim.32), channel_id=1, replica_groups=mesh['facet'=64,'pol'=4,'tm'=2] {'tm'}, dimensions={0} | all-to-all | bytes 2097152 | tf_op jit(solution)/shard_map/all_to_all | solution.py:33
  96.4 2.0 fusion.77
  98.4 2.0 fusion.78
  100.9 4.7 %all_to_all.38 = bf16[2,2,256,512]{3,2,1,0:T(8,128)(2,1)S(1)} all-to-all(bf16[2,2,256,512]{3,2,1,0:T(8,128)(2,1)S(1)} %broadcast_in_dim.33), channel_id=1, replica_groups=mesh['facet'=64,'pol'=4,'tm'=2] {'tm'}, dimensions={0} | all-to-all | bytes 2097152 | tf_op jit(solution)/shard_map/all_to_all | solution.py:33
  105.6 8.5 %fusion.74 = (bf16[1,1,512,512]{3,2,1,0:T(8,128)(2,1)S(1)}, bf16[1,1,512,512]{3,2,1,0:T(8,128)(2,1)S(1)}, bf16[1,1,512,512]{3,2,1,0:T(8,128)(2,1)S(1)}, bf16[1,1,512,512]{3,2,1,0:T(8,128)(2,1)S(1)}) fusion(bf16[1,512,512]{2,1,0:T(8,128)(2,1)S(1)} %bitcast.376, f32[512]{0:T(512)S(1)} %convert_multiply_fusion.8, bf16[1,512,512]{2,1,0:T(8,128)(2,1)S(1)} %bitcast.375), kind=kLoop, calls=%fused_computation.121 | loop fusion | flops 5505024 | bytes 3147776 | tf_op jit(solution)/shard_map/stack | solution.py:76
  114.1 0.7 fusion.39
  114.9 0.7 copy.75
  115.6 4.8 %all-to-all-start.3 = ((f32[1,2,128]{1,0,2:T(1,128)}), f32[1,2,128]{1,0,2:T(1,128)S(1)}, u32[]{:S(2)}, u32[]{:S(2)}) async-start(f32[1,2,128]{1,0,2:T(1,128)} %copy.75), calls=%async_computation.3 | async-start | bytes 131072 | tf_op jit(solution)/shard_map/all_to_all | solution.py:211
  120.5 0.7 gather_fusion.3
  121.9 3.0 %all-to-all-done.3 = f32[1,2,128]{1,0,2:T(1,128)S(1)} async-done(((f32[1,2,128]{1,0,2:T(1,128)}), f32[1,2,128]{1,0,2:T(1,128)S(1)}, u32[]{:S(2)}, u32[]{:S(2)}) %all-to-all-start.3) | async-done | bytes 1056 | tf_op jit(solution)/shard_map/all_to_all | solution.py:211
  125.2 136.7 %all-gather = f32[512,32,11]{1,2,0:T(8,128)S(1)} all-gather(f32[1,32,11]{1,2,0:T(8,128)S(1)} %maximum_bitcast_fusion), channel_id=1, replica_groups=mesh['facet'=64,'pol'=4,'tm'=2] {'facet','pol','tm'}, dimensions={0}, use_global_device_ids=true | all-gather | bytes 722304 | tf_op jit(solution)/shard_map/all_gather | solution.py:241
  261.9 0.9 copy.79
  262.8 2.3 reshape.946
  265.1 1.5 copy.93
  266.7 19.9 %while.11 = (s32[]{:T(128)}, f32[1,4,256]{2,1,0:T(4,128)S(1)}, f32[64,11,256]{2,0,1:T(8,128)S(1)}, f32[1]{0:T(128)}, s32[]{:T(128)}, /*index=5*/s32[]{:T(128)}, s32[]{}, s32[]{}, s32[]{}, s32[]{}) while((s32[]{:T(128)}, f32[1,4,256]{2,1,0:T(4,128)S(1)}, f32[64,11,256]{2,0,1:T(8,128)S(1)}, f32[1]{0:T(128)}, s32[]{:T(128)}, ...), condition=%wide.region_7.9_spmd.clone, body=%wide.region_6.8_spmd.clone.sunk | while | flops 1644807 | bytes 44223 | solution.py:259
  286.8 0.7 mul.845
  (411 shorter events, 30.8 us)
Async XLA Ops:
  0.6 113.4 %copy-start = (bf16[1,1,128,512]{3,2,1,0:T(8,128)(2,1)S(1)}, bf16[1,1,128,512]{3,2,1,0:T(8,128)(2,1)}, u32[]{:S(2)}) copy-start(bf16[1,1,128,512]{3,2,1,0:T(8,128)(2,1)} %param.22) | copy-start | bytes 393220
  12.3 21.2 %copy-start.2 = (bf16[1,1,128,512]{3,2,1,0:T(8,128)(2,1)S(1)}, bf16[1,1,128,512]{3,2,1,0:T(8,128)(2,1)}, u32[]{:S(2)}) copy-start(bf16[1,1,128,512]{3,2,1,0:T(8,128)(2,1)} %param.21) | copy-start | bytes 393220
  12.3 21.2 %copy-start.8 = (s32[1,1,3,8]{3,1,2,0:T(1,128)S(1)}, s32[1,1,3,8]{3,1,2,0:T(1,128)}, u32[]{:S(2)}) copy-start(s32[1,1,3,8]{3,1,2,0:T(1,128)} %param.25) | copy-start | bytes 292
  13.7 75.6 %all-to-all-start = ((bf16[64,1,32,128]{3,2,1,0:T(8,128)(2,1)}), bf16[64,1,32,128]{3,2,1,0:T(8,128)(2,1)}, u32[]{:S(2)}, u32[]{:S(2)}) async-start(bf16[64,1,32,128]{3,2,1,0:T(8,128)(2,1)} %copy.72), calls=%async_computation | async-start | bytes 1048576 | tf_op jit(solution)/shard_map/all_to_all | solution.py:188
  33.5 8.0 %copy-start.1 = (f32[256,4,512]{2,1,0:T(4,128)S(1)}, f32[256,4,512]{2,1,0:T(4,128)}, u32[]{:S(2)}) copy-start(f32[256,4,512]{2,1,0:T(4,128)} %param.27) | copy-start | bytes 6291460
  41.5 35.1 %copy-start.11 = (s32[4]{0:T(128)S(1)}, s32[4]{0:T(128)}, u32[]{:S(2)}) copy-start(s32[4]{0:T(128)} %constant.187) | copy-start | bytes 52
  41.5 35.7 %copy-start.10 = (s32[4]{0:T(128)S(1)}, s32[4]{0:T(128)}, u32[]{:S(2)}) copy-start(s32[4]{0:T(128)} %constant.189) | copy-start | bytes 52
  87.5 0.7 copy-start.13
  87.5 1.2 copy-start.6
  114.1 0.8 copy-start.9
  114.1 6.4 %copy-start.3 = (f32[32,4]{1,0:T(8,128)S(1)}, f32[32,4]{1,0:T(8,128)}, u32[]{:S(2)}) copy-start(f32[32,4]{1,0:T(8,128)} %gather_fusion.2) | copy-start | bytes 1540
  114.1 7.8 %copy-start.12 = (s32[32]{0:T(128)S(1)}, s32[32]{0:T(128)}, u32[]{:S(2)}) copy-start(s32[32]{0:T(128)} %get-tuple-element.68) | copy-start | bytes 388
  114.1 10.9 %copy-start.4 = (f32[4,1,32]{2,1,0:T(1,128)S(1)}, f32[4,1,32]{2,1,0:T(1,128)}, u32[]{:S(2)}) copy-start(f32[4,1,32]{2,1,0:T(1,128)} %get-tuple-element.107) | copy-start | bytes 1540
  114.1 11.0 %copy-start.5 = (f32[3,32]{1,0:T(4,128)S(1)}, f32[3,32]{1,0:T(4,128)}, u32[]{:S(2)}) copy-start(f32[3,32]{1,0:T(4,128)} %add_convert_fusion) | copy-start | bytes 1156
  115.6 9.3 %all-to-all-start.3 = ((f32[1,2,128]{1,0,2:T(1,128)}), f32[1,2,128]{1,0,2:T(1,128)S(1)}, u32[]{:S(2)}, u32[]{:S(2)}) async-start(f32[1,2,128]{1,0,2:T(1,128)} %copy.75), calls=%async_computation.3 | async-start | bytes 131072 | tf_op jit(solution)/shard_map/all_to_all | solution.py:211
  265.1 1.6 copy-start.7
where the time goes:
time: 289 us; the launch traced here: 288 us
  blocking collectives  146 us (51%)
  local copies, waits for them, and re-layouts  55.6 us (19%)
  matrix products  30.4 us (11%)
  other arithmetic  24.8 us (9%)
  starting transfers between devices  24.5 us (8%)
  waiting for transfers between devices  3 us (1%)
    all_gather x1, blocking collectives, on_device(): piece = lax.all_gather(records, ('facet', 'pol', 'tm'), axis=1, tiled=True)  137 us
    unnamed x31, local copies, waits for them, and re-layouts  34.2 us
    all_to_all x1, starting transfers between devices, on_device(): lax.all_to_all(contrib, 'facet', split_axis=0, concat_axis=1, tiled=True)  19.7 us
    dot_general x64, matrix products, one_group(): jnp.dot(jnp.transpose(weighted.reshape(group, own_count * 4)), onehot, pr...  14.9 us
    all_to_all x2, blocking collectives, from_everyone(): return lax.all_to_all(copies, axis, split_axis=0, concat_axis=0, tiled=True)  9.78 us
    another operation x1, other arithmetic, make_planes(): jnp.stack([sub_real * cosine - sub_imag * sine_part, sub_real * sine_part...  8.45 us
  transfers between devices with their start and end apart: 2, of which 1 were waited for; matrix products, arithmetic and copies ran while one was open for 20% of the time, Pallas kernels for 0%

commit v1 on v0

v1 whole, which is shorter than its diff:
```python
import functools
import math

import jax
import jax.numpy as jnp
import ml_dtypes
import numpy as np
from jax import lax
from jax.experimental import pallas as pl
from jax.experimental.pallas import tpu as pltpu
from jax.sharding import PartitionSpec as P

FGRID = 8
FS = 4096
MC = 64
SG = 512
NPOL = 4
NW = 2
NCH = 256
NST = 512
VT = 128
NBLK = 8
LINK_WINDOW = 256

w_chirp = 0.37
grad_scale = 0.1
MIB = 1 << 20

bf16 = jnp.bfloat16
f32 = jnp.float32
NT = (((1,), (1,)), ((), ()))


def dot_nt(left, right):
    return lax.dot_general(left, right, NT, preferred_element_type=f32)


def np_bf16(table):
    return np.asarray(table, np.float64).astype(np.float32).astype(ml_dtypes.bfloat16)


@functools.cache
def section_tables():
    a = np.arange(32)
    angle = -2 * np.pi * ((a[:, None] * a[None, :]) % 32) / 32
    c, s = np.cos(angle), np.sin(angle)
    first = np.block([[c, -s], [s, c]])
    k = np.arange(64)[:, None]
    l = np.arange(128)[None, :]
    turn = -2 * np.pi * ((k * l) % FS) / FS
    sub = np.arange(64)[:, None]
    angle = -2 * np.pi * ((sub * l) % 64) / 64
    last = np.concatenate([np.cos(angle), np.sin(angle)], axis=1) / math.sqrt(FS)
    return (
        np_bf16(first),
        np.stack([np.cos(turn), np.sin(turn)]).astype(np.float32),
        np_bf16(last),
    )


@functools.cache
def taper_tables():
    x = np.arange(SG)
    angle = 2 * np.pi * ((x[:, None] * x[None, :]) % SG) / SG
    table = np.exp(1j * angle) / math.sqrt(SG)
    across = (x - SG // 2) ** 2 * (w_chirp / SG**2)
    trailing, leading = [], []
    for w in range(NW):
        full = table * np.exp(2j * np.pi * w * across)[None, :]
        rows = np.stack([full.real, -full.imag]).reshape(2, FGRID, MC, SG)
        trailing.append(rows.transpose(1, 0, 2, 3).reshape(2 * SG, SG))
        halves = np.stack([full.real, full.imag]).reshape(2, FGRID, 2, MC // 2, SG)
        leading.append(halves.transpose(2, 0, 1, 3, 4).reshape(2, 2 * SG // 2, SG))
    return np_bf16(np.stack(trailing)), np_bf16(np.stack(leading, axis=1))


def contrib_kernel(x_ref, u_ref, v_ref, w_ref, first_ref, turn_ref, last_ref, out_ref, pack_ref, spread, lined, placed):
    rows = x_ref.shape[1]
    pack_ref[0:VT, :] = u_ref[...]
    pack_ref[VT : 2 * VT, :] = v_ref[...]
    pack_ref[2 * VT : 2 * VT + 16, :] = jnp.zeros((16, SG), bf16)
    pack_ref[2 * VT : 2 * VT + 16, 0:VT] = w_ref[...]
    for part in range(2):
        for a in range(32):
            at = (part * 32 + a) * rows
            spread[at : at + rows, :] = x_ref[part, :, a * 128 : (a + 1) * 128].astype(f32)
    for m in range(rows):
        lined[:, m * 128 : (m + 1) * 128] = spread[pl.ds(m, 64, stride=rows), :].astype(bf16)
    turn_re = turn_ref[0]
    turn_im = turn_ref[1]
    for pair in range(rows // 2):
        section = jnp.dot(
            first_ref[...], lined[:, pair * 256 : (pair + 1) * 256], preferred_element_type=f32
        )
        sides = []
        for half in range(2):
            one = section[:, half * 128 : (half + 1) * 128]
            re = jnp.concatenate([one[0:32], one[0:32]], axis=0)
            im = jnp.concatenate([one[32:64], one[32:64]], axis=0)
            turned_re = (re * turn_re - im * turn_im).astype(bf16)
            turned_im = (re * turn_im + im * turn_re).astype(bf16)
            sides.append(
                jnp.concatenate(
                    [
                        jnp.concatenate([turned_re, -turned_im], axis=1),
                        jnp.concatenate([turned_im, turned_re], axis=1),
                    ],
                    axis=0,
                )
            )
        result = dot_nt(last_ref[...], jnp.concatenate(sides, axis=0))
        placed[pl.ds(2 * pair, 64, stride=rows), :] = result[:, 0:128]
        placed[pl.ds(2 * pair + 1, 64, stride=rows), :] = result[:, 128:256]
    for s in range(64):
        out_ref[s] = placed[s * rows : (s + 1) * rows, :].astype(bf16)


def contributions(x, u, v, w):
    rows = x.shape[1]
    first, turn, last = section_tables()
    return pl.pallas_call(
        contrib_kernel,
        out_shape=(
            jax.ShapeDtypeStruct((64, rows, 128), bf16),
            jax.ShapeDtypeStruct((2 * VT + 16, SG), bf16),
        ),
        scratch_shapes=[
            pltpu.VMEM((64 * rows, 128), f32),
            pltpu.VMEM((64, 128 * rows), bf16),
            pltpu.VMEM((64 * rows, 128), f32),
        ],
        compiler_params=pltpu.CompilerParams(vmem_limit_bytes=16 * MIB),
        cost_estimate=pl.CostEstimate(flops=300_000_000, bytes_accessed=2 * MIB, transcendentals=0),
        name="contrib",
    )(x, u, v, w, jnp.asarray(first), jnp.asarray(turn), jnp.asarray(last))


def taper_kernel(sc_ref, u_ref, v_ref, w_ref, other_ref, trail_ref, lead_ref, b_ref, a_ref):
    del sc_ref
    v_all = jnp.concatenate([v_ref[...], other_ref[VT : 2 * VT, :]], axis=0)
    u_all = jnp.concatenate([u_ref[...], other_ref[0:VT, :]], axis=0)
    weights = jnp.concatenate([w_ref[...], other_ref[2 * VT : 2 * VT + 16, 0:VT]], axis=1).astype(f32)
    for w in range(NW):
        re_at = slice(w * 256, (w + 1) * 256)
        im_at = slice(512 + w * 256, 512 + (w + 1) * 256)
        for j in range(FGRID):
            got = dot_nt(trail_ref[w, j * 128 : (j + 1) * 128, :], v_all)
            b_ref[j * 128 : (j + 1) * 128, re_at] = got.astype(bf16)
            b_ref[j * 128 : j * 128 + 64, im_at] = (-got[64:128]).astype(bf16)
            b_ref[j * 128 + 64 : (j + 1) * 128, im_at] = got[0:64].astype(bf16)
        scale = weights[w : w + 1, :]
        a_ref[0, :, re_at] = dot_nt(lead_ref[w, 0:256, :], u_all) * scale
        a_ref[1, :, re_at] = dot_nt(lead_ref[w, 256:512, :], u_all) * scale


def taper_transforms(where, u, v, w, other):
    trailing, leading = taper_tables()
    whole = lambda shape: pl.BlockSpec(shape, lambda i, sc: (0,) * len(shape))
    return pl.pallas_call(
        taper_kernel,
        out_shape=(
            jax.ShapeDtypeStruct((2 * SG, 1024), bf16),
            jax.ShapeDtypeStruct((2, SG // 2, 512), f32),
        ),
        grid_spec=pltpu.PrefetchScalarGridSpec(
            num_scalar_prefetch=1,
            grid=(1,),
            in_specs=[
                whole((VT, SG)),
                whole((VT, SG)),
                whole((16, VT)),
                whole((2 * VT + 16, SG)),
                whole((NW, 2 * SG, SG)),
                pl.BlockSpec((None, NW, SG, SG), lambda i, sc: (sc[2], 0, 0, 0)),
            ],
            out_specs=(whole((2 * SG, 1024)), whole((2, SG // 2, 512))),
        ),
        compiler_params=pltpu.CompilerParams(vmem_limit_bytes=24 * MIB),
        cost_estimate=pl.CostEstimate(flops=800_000_000, bytes_accessed=8 * MIB, transcendentals=0),
        name="tapers",
    )(where, u, v, w, other, jnp.asarray(trailing), jnp.asarray(leading))


def slots_kernel(sc_ref, table_ref, obs_ref, links_ref, gains_ref, out_ref, window, factors, link_sem, gain_sem):
    tiles = links_ref.shape[1] // 128
    begin = jnp.int32(0)
    blocks = []
    copies = []
    for b in range(NBLK):
        channel = table_ref[0, b]
        offset = table_ref[1, b]
        amount = table_ref[2, b]
        tile = jnp.minimum(offset // 128, tiles - LINK_WINDOW // 128)
        at = pl.multiple_of(tile * 128, 128)
        copies.append(
            pltpu.make_async_copy(links_ref.at[:, pl.ds(at, LINK_WINDOW)], window.at[b], link_sem.at[b])
        )
        copies.append(pltpu.make_async_copy(gains_ref.at[channel], factors.at[b], gain_sem.at[b]))
        blocks.append((channel, offset - at, amount, begin))
        begin = begin + amount
    for copy in copies:
        copy.start()
    slot = lax.broadcasted_iota(jnp.int32, (1, VT), 1)
    members = []
    chooser = []
    live = jnp.zeros((1, VT), f32)
    channels = jnp.zeros((1, VT), f32)
    index = lax.broadcasted_iota(jnp.int32, (LINK_WINDOW, VT), 0)
    for channel, shift, amount, start in blocks:
        inside = (slot >= start) & (slot < start + amount)
        member = jnp.where(inside, 1.0, 0.0)
        members.append(member)
        live = live + member
        channels = channels + member * channel.astype(f32)
        want = jnp.where(inside, slot - start + shift, -1)
        chooser.append(jnp.where(index == want, 1.0, 0.0).astype(bf16))
    for copy in copies:
        copy.wait()
    digits = []
    for b in range(NBLK):
        found = window[b]
        high = found >> 4
        digits.append(jnp.concatenate([high, found - (high << 4)], axis=0).astype(f32).astype(bf16))
    picked = jnp.dot(
        jnp.concatenate(digits, axis=1), jnp.concatenate(chooser, axis=0), preferred_element_type=f32
    )
    stations = picked[0:2] * 16.0 + picked[2:4]
    both = jnp.concatenate([stations[0:1], stations[1:2]], axis=1).astype(jnp.int32)
    station_index = lax.broadcasted_iota(jnp.int32, (NST, 2 * VT), 0)
    onehot = jnp.where(station_index == both, 1.0, 0.0).astype(bf16)
    rest = jnp.concatenate([factors[b] for b in range(NBLK)], axis=0)
    taken = jnp.zeros((4 * NBLK, 2 * VT), f32)
    for piece in range(3):
        rounded = rest.astype(bf16)
        taken = taken + jnp.dot(rounded, onehot, preferred_element_type=f32)
        rest = rest - rounded.astype(f32)
    gain_first = jnp.zeros((4, VT), f32)
    gain_second = jnp.zeros((4, VT), f32)
    for b in range(NBLK):
        gain_first = gain_first + members[b] * taken[4 * b : 4 * b + 4, 0:VT]
        gain_second = gain_second + members[b] * taken[4 * b : 4 * b + 4, VT : 2 * VT]
    quarter = obs_ref.shape[3]
    lane = lax.broadcasted_iota(jnp.int32, (1, VT), 1)
    mine = (lane // quarter) == sc_ref[1]
    out_ref[0:4, :] = jnp.zeros((4, VT), f32)
    for row in range(2 * NPOL):
        one = obs_ref[0, row]
        spread = jnp.concatenate([one] * (VT // quarter), axis=1)
        out_ref[4 + row : 5 + row, :] = jnp.where(mine, spread, 0.0)
    out_ref[12:16, :] = gain_first
    out_ref[16:20, :] = gain_second
    out_ref[20:22, :] = stations
    out_ref[22:23, :] = channels
    out_ref[23:24, :] = live


def slot_rows(where, table, observed, links, gains):
    smem = pl.BlockSpec(memory_space=pltpu.SMEM)
    anywhere = pl.BlockSpec(memory_space=pl.ANY)
    return pl.pallas_call(
        slots_kernel,
        out_shape=jax.ShapeDtypeStruct((24, VT), f32),
        in_specs=[smem, smem, pl.BlockSpec(memory_space=pltpu.VMEM), anywhere, anywhere],
        out_specs=pl.BlockSpec(memory_space=pltpu.VMEM),
        scratch_shapes=[
            pltpu.VMEM((NBLK, 2, LINK_WINDOW), jnp.int32),
            pltpu.VMEM((NBLK, 4, NST), f32),
            pltpu.SemaphoreType.DMA((NBLK,)),
            pltpu.SemaphoreType.DMA((NBLK,)),
        ],
        compiler_params=pltpu.CompilerParams(vmem_limit_bytes=8 * MIB),
        cost_estimate=pl.CostEstimate(flops=50_000_000, bytes_accessed=2 * MIB, transcendentals=0),
        name="slots",
    )(where, table, observed, links, gains)


def predict_kernel(sc_ref, got_ref, b_ref, a_ref, info_ref, out_ref):
    rows = got_ref.shape[1]
    left = jnp.concatenate(
        [
            jnp.concatenate([got_ref[i * FGRID + j] for j in range(FGRID)], axis=1)
            for i in range(FGRID)
        ],
        axis=0,
    )
    del rows
    total_re = [jnp.zeros((1, VT), f32), jnp.zeros((1, VT), f32)]
    total_im = [jnp.zeros((1, VT), f32), jnp.zeros((1, VT), f32)]
    for w in range(NW):
        at = slice(w * 256, (w + 1) * 256)
        along_re = jnp.dot(left, b_ref[:, w * 256 : (w + 1) * 256], preferred_element_type=f32)
        along_im = jnp.dot(left, b_ref[:, 512 + w * 256 : 512 + (w + 1) * 256], preferred_element_type=f32)
        a_re = a_ref[0, :, at]
        a_im = a_ref[1, :, at]
        sum_re = jnp.sum(a_re * along_re - a_im * along_im, axis=0, keepdims=True)
        sum_im = jnp.sum(a_re * along_im + a_im * along_re, axis=0, keepdims=True)
        for side in range(2):
            total_re[side] = total_re[side] + sum_re[:, side * VT : (side + 1) * VT]
            total_im[side] = total_im[side] + sum_im[:, side * VT : (side + 1) * VT]
    first = sc_ref[2] == 0
    rows_out = [
        jnp.where(first, total_re[0], total_re[1]),
        jnp.where(first, total_re[1], total_re[0]),
        jnp.where(first, total_im[0], total_im[1]),
        jnp.where(first, total_im[1], total_im[0]),
    ]
    head = jnp.concatenate(rows_out + [info_ref[4:8, :]], axis=0)
    for to in range(out_ref.shape[0]):
        out_ref[to, 0:8, :] = head
        out_ref[to, 8:24, :] = info_ref[8:24, :]


def partial_predictions(where, got, b, a, info, peers):
    vmem = pl.BlockSpec(memory_space=pltpu.VMEM)
    return pl.pallas_call(
        predict_kernel,
        out_shape=jax.ShapeDtypeStruct((peers, 24, VT), f32),
        in_specs=[pl.BlockSpec(memory_space=pltpu.SMEM), vmem, vmem, vmem, vmem],
        out_specs=vmem,
        compiler_params=pltpu.CompilerParams(vmem_limit_bytes=20 * MIB),
        cost_estimate=pl.CostEstimate(flops=540_000_000, bytes_accessed=4 * MIB, transcendentals=0),
        name="predict",
    )(where, got, b, a, info)


def gradient_kernel(sc_ref, got_ref, resid_ref, out_ref):
    owners = 2
    own_class = sc_ref[1] * owners + sc_ref[2]
    row_id = lax.broadcasted_iota(jnp.int32, (SG, VT), 0)
    lane_of = lax.broadcasted_iota(jnp.int32, (VT, VT), 0)
    pick = lambda rows, order: jnp.concatenate([rows[i : i + 1] for i in order], axis=0)
    masks = {}
    values = {}
    resid_owner = []
    for o in range(owners):
        info = got_ref[o]
        measured = got_ref[o, 4:12, :]
        for p in range(1, NPOL):
            measured = measured + got_ref[p * owners + o, 4:12, :]
        pred_re = []
        pred_im = []
        for p in range(NPOL):
            one, two = got_ref[p * owners], got_ref[p * owners + 1]
            pred_re.append(one[o : o + 1] + two[o : o + 1])
            pred_im.append(one[2 + o : 3 + o] + two[2 + o : 3 + o])
        pred_re = jnp.concatenate(pred_re, axis=0)
        pred_im = jnp.concatenate(pred_im, axis=0)
        gain_first = info[12:16]
        gain_second = info[16:20]
        live = info[23:24]
        first_re = pick(gain_first, (0, 0, 2, 2))
        first_im = pick(gain_first, (1, 1, 3, 3))
        second_re = pick(gain_second, (0, 2, 0, 2))
        second_im = pick(gain_second, (1, 3, 1, 3))
        obs_re = pick(measured, (0, 2, 4, 6))
        obs_im = pick(measured, (1, 3, 5, 7))
        both_re = first_re * second_re + first_im * second_im
        both_im = first_im * second_re - first_re * second_im
        resid_re = live * (obs_re - (both_re * pred_re - both_im * pred_im))
        resid_im = live * (obs_im - (both_re * pred_im + both_im * pred_re))
        cross_re = second_re * pred_re + second_im * pred_im
        cross_im = second_im * pred_re - second_re * pred_im
        lead_re = -(resid_re * cross_re - resid_im * cross_im)
        lead_im = -(resid_re * cross_im + resid_im * cross_re)
        along_re = first_re * pred_re - first_im * pred_im
        along_im = first_re * pred_im + first_im * pred_re
        trail_re = -(resid_re * along_re + resid_im * along_im)
        trail_im = -(resid_re * along_im - resid_im * along_re)
        leading = jnp.concatenate(
            [
                lead_re[0:1] + lead_re[1:2],
                lead_im[0:1] + lead_im[1:2],
                lead_re[2:3] + lead_re[3:4],
                lead_im[2:3] + lead_im[3:4],
            ],
            axis=0,
        )
        trailing = jnp.concatenate(
            [
                trail_re[0:1] + trail_re[2:3],
                trail_im[0:1] + trail_im[2:3],
                trail_re[1:2] + trail_re[3:4],
                trail_im[1:2] + trail_im[3:4],
            ],
            axis=0,
        )
        resid_owner.append(
            jnp.concatenate(
                [r for p in range(NPOL) for r in (resid_re[p : p + 1], resid_im[p : p + 1])], axis=0
            )
        )
        channel = info[22:23].astype(jnp.int32)
        chosen = (lane_of >> 2) == (channel & 31)
        for side, terms in ((0, leading), (1, trailing)):
            station = info[20 + side : 21 + side].astype(jnp.int32)
            key = jnp.where((station & 7) == own_class, (station >> 3) * 8 + (channel >> 5), -1)
            masks[side, o] = jnp.where(row_id == key, 1.0, 0.0).astype(bf16)
            tall = jnp.concatenate([terms, terms], axis=0)
            tall = jnp.concatenate([tall] * 16, axis=0)
            values[side, o] = jnp.where(chosen, tall, 0.0).astype(bf16)
    order = [(side, o) for side in range(2) for o in range(owners)]
    mask = jnp.concatenate([masks[at] for at in order], axis=1)
    value = jnp.concatenate([values[at] for at in order], axis=1)
    out_ref[...] = dot_nt(mask, value).astype(bf16)
    mine = jnp.where(sc_ref[2] == 0, resid_owner[0], resid_owner[1])
    quarter = resid_ref.shape[3]
    part = mine[:, 0:quarter]
    for q in range(1, NPOL):
        part = jnp.where(sc_ref[1] == q, mine[:, q * quarter : (q + 1) * quarter], part)
    for row in range(2 * NPOL):
        resid_ref[0, row] = part[row : row + 1, :]


def gradient_rows(where, got, quarter):
    vmem = pl.BlockSpec(memory_space=pltpu.VMEM)
    return pl.pallas_call(
        gradient_kernel,
        out_shape=(
            jax.ShapeDtypeStruct((1, 2 * NPOL, 1, quarter), f32),
            jax.ShapeDtypeStruct((SG, 128), bf16),
        ),
        in_specs=[pl.BlockSpec(memory_space=pltpu.SMEM), vmem],
        out_specs=(vmem, vmem),
        compiler_params=pltpu.CompilerParams(vmem_limit_bytes=12 * MIB),
        cost_estimate=pl.CostEstimate(flops=70_000_000, bytes_accessed=MIB, transcendentals=0),
        name="gradient",
    )(where, got)


def on_device(
    tile_spectral_lines,
    taper_leading_axis,
    taper_trailing_axis,
    depth_layer_factors,
    measured_correlations,
    visibility_groups_table,
    antenna_links,
    complex_receiver_factors,
):
    where = jnp.stack([lax.axis_index("facet"), lax.axis_index("pol"), lax.axis_index("tm")]).astype(jnp.int32)
    quarter = measured_correlations.shape[3]
    u = taper_leading_axis.reshape(VT, SG)
    v = taper_trailing_axis.reshape(VT, SG)
    w = jnp.pad(depth_layer_factors.reshape(NW, VT), ((0, 16 - NW), (0, 0)))
    x = tile_spectral_lines.reshape(tile_spectral_lines.shape[2:])
    contrib, pack = contributions(x, u, v, w)
    received = lax.all_to_all(contrib, "facet", split_axis=0, concat_axis=0, tiled=True)
    other = lax.ppermute(pack, "tm", [(0, 1), (1, 0)])
    b, a = taper_transforms(where, u, v, w, other)
    info = slot_rows(
        where,
        visibility_groups_table.reshape(3, NBLK),
        measured_correlations,
        antenna_links,
        complex_receiver_factors,
    )
    peers = lax.axis_size(("pol", "tm"))
    sent = partial_predictions(where, received, b, a, info, peers)
    gathered = lax.all_to_all(sent, ("pol", "tm"), split_axis=0, concat_axis=0, tiled=True)
    residual, partial_rows = gradient_rows(where, gathered, quarter)
    rows = lax.all_to_all(
        partial_rows.reshape(64, 8, 128), "facet", split_axis=0, concat_axis=0, tiled=True
    )
    gain_grad = grad_scale * jnp.sum(rows.astype(f32), axis=0)
    return (residual, gain_grad.reshape(1, 4 * NCH))


def solution(mesh):
    return jax.shard_map(
        on_device,
        mesh=mesh,
        in_specs=(
            P("facet", "pol", None, "tm", None),
            P("facet", "tm", None, None),
            P("facet", "tm", None, None),
            P("facet", "tm", None, None),
            P("facet", None, "tm", "pol"),
            P("facet", "tm", None, None),
            P(),
            P(),
        ),
        out_specs=(P("facet", None, "tm", "pol"), P(("facet", "pol", "tm"), None)),
        check_vma=False,
    )
```

time: 289 us -> 99.2 us (0.34)
  blocking collectives: 146 us -> 33.2 us
  local copies, waits for them, and re-layouts: 55.6 us -> 11.1 us
  matrix products: 30.4 us -> 0 us
  other arithmetic: 24.8 us -> 0.75 us
  waiting for transfers between devices: 3 us -> 19.2 us
  Pallas kernels: 0 us -> 10.2 us
    all_gather x1 -> x0, blocking collectives: 137 us -> none  [on_device(): piece = lax.all_gather(records, ('facet', 'pol', 'tm'), axis=1, tiled=True)]
    dot_general x76 -> x0, matrix products: 30.4 us -> none  [the longest x64 14.9 us: one_group(): jnp.dot(jnp.transpose(weighted.reshape(group, own_count * 4)), onehot, pr...]
    unnamed x31 -> x33, local copies, waits for them, and re-layouts: 34.2 us -> 10.3 us
    all_to_all x2, blocking collectives: 9.78 us -> 33.2 us  [the longest x1 20.3 us: on_device(): lax.all_to_all(partial_rows.reshape(64, 8, 128), 'facet', split_axis=0, c...]
    all_to_all x2 -> x1, waiting for transfers between devices: 3 us -> 19.2 us  [on_device(): lax.all_to_all(contrib, 'facet', split_axis=0, concat_axis=0, tiled=True)]
    pallas_call x0 -> x5, Pallas kernels: none -> 10.2 us  [the longest x1 3.58 us: contributions(): pl.pallas_call(contrib_kernel, out_shape=(jax.ShapeDtypeStruct((64, rows,...]
    another operation x9 -> x1, other arithmetic: 9.23 us -> 0.08 us  [on_device(): jnp.stack([lax.axis_index('facet'), lax.axis_index('pol'), lax.axis_index...]
    gather x10 -> x0, local copies, waits for them, and re-layouts: 7.38 us -> none  [the longest x2 2.01 us: on_device(): gain_second = gains_turned[channel, antenna_right]]
  transfers between devices with their start and end apart: 2 -> 2, of which waited for: 1 -> 1; matrix products, arithmetic and copies ran while one was open for 20% -> 0% of each run, Pallas kernels for 0% -> 4%
where the time goes in v1:
time: 99.2 us; the launch traced here: 97.3 us
  blocking collectives  33.2 us (33%)
  starting transfers between devices  22.1 us (22%)
  waiting for transfers between devices  19.2 us (19%)
  local copies, waits for them, and re-layouts  11.1 us (11%)
  Pallas kernels  10.2 us (10%)
    all_to_all x1, blocking collectives, on_device(): lax.all_to_all(partial_rows.reshape(64, 8, 128), 'facet', split_axis=0, c...  20.3 us
    all_to_all x1, starting transfers between devices, on_device(): lax.all_to_all(contrib, 'facet', split_axis=0, concat_axis=0, tiled=True)  19.3 us
    all_to_all x1, waiting for transfers between devices, on_device(): lax.all_to_all(contrib, 'facet', split_axis=0, concat_axis=0, tiled=True)  19.2 us
    all_to_all x1, blocking collectives, on_device(): lax.all_to_all(sent, ('pol', 'tm'), split_axis=0, concat_axis=0, tiled=True)  12.8 us
    unnamed x33, local copies, waits for them, and re-layouts  10.3 us
    pallas_call x1, Pallas kernels, contributions(): pl.pallas_call(contrib_kernel, out_shape=(jax.ShapeDtypeStruct((64, rows,...  3.58 us
    ppermute x1, starting transfers between devices, on_device(): other = lax.ppermute(pack, 'tm', [(0, 1), (1, 0)])  2.86 us
    pallas_call x1, Pallas kernels, taper_transforms(): pl.pallas_call(taper_kernel, out_shape=(jax.ShapeDtypeStruct((2 * SG, 102...  2.33 us
  transfers between devices with their start and end apart: 2, of which 1 were waited for; matrix products, arithmetic and copies ran while one was open for 0% of the time, Pallas kernels for 4%

profile of v1, /device:TPU:1, one launch (start us, length us, event | category | flops | bytes accessed | tf_op | source)
XLA Modules:
  0.0 97.3 jit_solution(2663656116456342013)
XLA Ops:
  0.6 0.0 copy-start
  0.6 0.8 pad.4.w_ref
  1.5 0.9 copy-done.6
  2.4 0.9 copy-done.8
  3.3 1.0 %copy-done.11 = bf16[1,1,2,32,4096]{4,3,2,1,0:T(8,128)(2,1)S(1)} copy-done((bf16[1,1,2,32,4096]{4,3,2,1,0:T(8,128)(2,1)S(1)}, bf16[1,1,2,32,4096]{4,3,2,1,0:T(8,128)(2,1)}, u32[]{:S(2)}) %copy-start.11) | copy-done | bytes 524312
  4.3 0.8 copy-done.12
  5.1 0.8 copy-done.13
  5.9 0.7 copy-done.14
  6.6 3.6 %contrib.1 = (bf16[64,32,128]{2,1,0:T(8,128)(2,1)}, bf16[272,512]{1,0:T(8,128)(2,1)S(1)}) custom-call(bf16[2,32,4096]{2,1,0:T(8,128)(2,1)S(1)} %bitcast.18, bf16[128,512]{1,0:T(8,128)(2,1)S(1)} %bitcast.12, bf16[128,512]{1,0:T(8,128)(2,1)S(1)} %bitcast.14, bf16[16,128]{1,0:T(8,128)(2,1)S(1)} %pad.4.w_ref, bf16[64,64]{1,0:T(8,128)(2,1)S(1)} %copy-done.14, ...), custom_call_target="tpu_custom_call" | custom-call | flops 300000000 | bytes 2097152 | tf_op jit(solution)/shard_map/contrib/pallas_call | solution.py:121
  10.2 19.3 %all-to-all-start = ((bf16[64,32,128]{2,1,0:T(8,128)(2,1)}), bf16[64,32,128]{2,1,0:T(8,128)(2,1)S(1)}, u32[]{:S(2)}, u32[]{:S(2)}) async-start(bf16[64,32,128]{2,1,0:T(8,128)(2,1)} %get-tuple-element.8), calls=%async_computation | async-start | bytes 1048576 | tf_op jit(solution)/shard_map/all_to_all | solution.py:447
  29.5 2.9 %collective-permute-start = (bf16[272,512]{1,0:T(8,128)(2,1)S(1)}, bf16[272,512]{1,0:T(8,128)(2,1)S(1)}, u32[]{:S(2)}, u32[]{:S(2)}) collective-permute-start(bf16[272,512]{1,0:T(8,128)(2,1)S(1)} %get-tuple-element.9), channel_id=1, source_target_pairs={{0,1},{1,0},{2,3},{3,2},{4,5},{5,4},{6,7},{7,6},{8,9},{9,8},{10,11... | collective-permute-start | bytes 835592 | tf_op jit(solution)/shard_map/ppermute | solution.py:448
  32.4 0.0 copy-start.1
  32.4 0.1 pad_add_fusion.sc_ref
  32.5 0.0 copy-done.10
  32.5 1.4 %copy-done.5 = s32[2,130816]{1,0:T(2,128)S(1)} copy-done((s32[2,130816]{1,0:T(2,128)S(1)}, s32[2,130816]{1,0:T(2,128)}, u32[]{:S(2)}) %copy-start.5) | copy-done | bytes 1046552
  33.8 1.5 %slots.1.info_ref = f32[24,128]{1,0:T(8,128)S(1)} custom-call(s32[3]{0:T(128)S(1)} %pad_add_fusion.sc_ref, s32[3,8]{1,0:T(4,128)S(1)} %bitcast.17, f32[1,8,1,32]{3,2,1,0:T(1,128)S(1)} %copy-done.10, s32[2,130816]{1,0:T(2,128)S(1)} %copy-done.5, f32[256,4,512]{2,1,0:T(4,128)S(1)} %copy-done), custom_call_target="tpu_custom_call" | custom-call | flops 50000000 | bytes 2097152 | tf_op jit(solution)/shard_map/slots/pallas_call | solution.py:260
  35.4 0.0 collective-permute-done.other_ref
  35.4 0.0 copy-done.1
  35.4 0.0 copy-done.7
  35.4 0.0 copy-done.9
  35.4 0.0 copy-start.2
  35.4 1.6 %copy-done.2 = bf16[2,2,512,512]{3,2,1,0:T(8,128)(2,1)S(1)} copy-done((bf16[2,2,512,512]{3,2,1,0:T(8,128)(2,1)S(1)}, bf16[2,2,512,512]{3,2,1,0:T(8,128)(2,1)}, u32[]{:S(2)}) %copy-start.2) | copy-done | bytes 2097176
  37.0 2.3 %tapers.1 = (bf16[1024,1024]{1,0:T(8,128)(2,1)S(1)}, f32[2,256,512]{2,1,0:T(8,128)S(1)}) custom-call(s32[3]{0:T(128)S(1)} %pad_add_fusion.sc_ref, bf16[128,512]{1,0:T(8,128)(2,1)S(1)} %bitcast.13, bf16[128,512]{1,0:T(8,128)(2,1)S(1)} %bitcast.15, bf16[16,128]{1,0:T(8,128)(2,1)S(1)} %pad.4.w_ref, bf16[272,512]{1,0:T(8,128)(2,1)S(1)} %collective-permute-done.other_ref, ...), custom_call_target="tpu_custom_call" | custom-call | flops 800000000 | bytes 8388608 | tf_op jit(solution)/shard_map/tapers/pallas_call | solution.py:159
  39.3 1.0 copy-done.3
  40.3 19.2 %all-to-all-done.got_ref = bf16[64,32,128]{2,1,0:T(8,128)(2,1)S(1)} async-done(((bf16[64,32,128]{2,1,0:T(8,128)(2,1)}), bf16[64,32,128]{2,1,0:T(8,128)(2,1)S(1)}, u32[]{:S(2)}, u32[]{:S(2)}) %all-to-all-start) | async-done | bytes 524320 | tf_op jit(solution)/shard_map/all_to_all | solution.py:447
  59.5 1.2 %copy-done.4 = f32[2,256,512]{2,1,0:T(8,128)S(1)} copy-done((f32[2,256,512]{2,1,0:T(8,128)S(1)}, f32[2,256,512]{2,1,0:T(8,128)}, u32[]{:S(2)}) %copy-start.4) | copy-done | bytes 1048600
  60.7 1.3 %predict.1 = f32[8,24,128]{2,1,0:T(8,128)S(1)} custom-call(s32[3]{0:T(128)S(1)} %pad_add_fusion.sc_ref, bf16[64,32,128]{2,1,0:T(8,128)(2,1)S(1)} %all-to-all-done.got_ref, bf16[1024,1024]{1,0:T(8,128)(2,1)S(1)} %get-tuple-element.10.b_ref, f32[2,256,512]{2,1,0:T(8,128)S(1)} %copy-done.4, f32[24,128]{1,0:T(8,128)S(1)} %slots.1.info_ref), custom_call_target="tpu_custom_call" | custom-call | flops 540000000 | bytes 4194304 | tf_op jit(solution)/shard_map/predict/pallas_call | solution.py:315
  62.0 12.8 %all_to_all.15.got_ref = f32[8,24,128]{2,1,0:T(8,128)S(1)} all-to-all(f32[8,24,128]{2,1,0:T(8,128)S(1)} %predict.1), channel_id=1, replica_groups=mesh['facet'=64,'pol'=4,'tm'=2] {'pol','tm'}, dimensions={0} | all-to-all | bytes 196608 | tf_op jit(solution)/shard_map/all_to_all | solution.py:459
  74.8 1.5 %gradient.1 = (f32[1,8,1,32]{3,2,1,0:T(1,128)}, bf16[512,128]{1,0:T(8,128)(2,1)S(1)}) custom-call(s32[3]{0:T(128)S(1)} %pad_add_fusion.sc_ref, f32[8,24,128]{2,1,0:T(8,128)S(1)} %all_to_all.15.got_ref), custom_call_target="tpu_custom_call" | custom-call | flops 70000000 | bytes 1048576 | tf_op jit(solution)/shard_map/gradient/pallas_call | solution.py:416
  76.3 20.3 %all_to_all.16 = bf16[64,8,128]{2,1,0:T(8,128)(2,1)S(1)} all-to-all(bf16[64,8,128]{2,1,0:T(8,128)(2,1)S(1)} %bitcast.16), channel_id=1, replica_groups=mesh['facet'=64,'pol'=4,'tm'=2] {'facet'}, dimensions={0} | all-to-all | bytes 262144 | tf_op jit(solution)/shard_map/all_to_all | solution.py:461
  96.7 0.1 convert_reduce_fusion
  96.7 0.6 broadcast_multiply_fusion
  (16 shorter events, 0.0 us)
Async XLA Ops:
  0.6 31.9 %copy-start = (f32[256,4,512]{2,1,0:T(4,128)S(1)}, f32[256,4,512]{2,1,0:T(4,128)}, u32[]{:S(2)}) copy-start(f32[256,4,512]{2,1,0:T(4,128)} %gains_ref.1) | copy-start | bytes 6291460
  1.5 0.9 copy-start.6
  2.4 0.9 copy-start.8
  3.3 1.0 %copy-start.11 = (bf16[1,1,2,32,4096]{4,3,2,1,0:T(8,128)(2,1)S(1)}, bf16[1,1,2,32,4096]{4,3,2,1,0:T(8,128)(2,1)}, u32[]{:S(2)}) copy-start(bf16[1,1,2,32,4096]{4,3,2,1,0:T(8,128)(2,1)} %param.13) | copy-start | bytes 1572868
  4.3 0.8 copy-start.12
  5.1 0.8 copy-start.13
  5.9 0.7 copy-start.14
  6.6 25.7 %copy-start.15 = (s32[1,1,3,8]{3,1,2,0:T(1,128)S(1)}, s32[1,1,3,8]{3,1,2,0:T(1,128)}, u32[]{:S(2)}) copy-start(s32[1,1,3,8]{3,1,2,0:T(1,128)} %param.18) | copy-start | bytes 292
  6.6 25.9 %copy-start.10 = (f32[1,8,1,32]{3,2,1,0:T(1,128)S(1)}, f32[1,8,1,32]{3,2,1,0:T(1,128)}, u32[]{:S(2)}) copy-start(f32[1,8,1,32]{3,2,1,0:T(1,128)} %obs_ref.1) | copy-start | bytes 3076
  10.2 49.3 %all-to-all-start = ((bf16[64,32,128]{2,1,0:T(8,128)(2,1)}), bf16[64,32,128]{2,1,0:T(8,128)(2,1)S(1)}, u32[]{:S(2)}, u32[]{:S(2)}) async-start(bf16[64,32,128]{2,1,0:T(8,128)(2,1)} %get-tuple-element.8), calls=%async_computation | async-start | bytes 1048576 | tf_op jit(solution)/shard_map/all_to_all | solution.py:447
  29.5 5.9 %collective-permute-start = (bf16[272,512]{1,0:T(8,128)(2,1)S(1)}, bf16[272,512]{1,0:T(8,128)(2,1)S(1)}, u32[]{:S(2)}, u32[]{:S(2)}) collective-permute-start(bf16[272,512]{1,0:T(8,128)(2,1)S(1)} %get-tuple-element.9), channel_id=1, source_target_pairs={{0,1},{1,0},{2,3},{3,2},{4,5},{5,4},{6,7},{7,6},{8,9},{9,8},{10,11... | collective-permute-start | bytes 835592 | tf_op jit(solution)/shard_map/ppermute | solution.py:448
  32.4 3.0 %copy-start.1 = (bf16[2,1024,512]{2,1,0:T(8,128)(2,1)S(1)}, bf16[2,1024,512]{2,1,0:T(8,128)(2,1)}, u32[]{:S(2)}) copy-start(bf16[2,1024,512]{2,1,0:T(8,128)(2,1)} %constant.33.clone.trail_ref) | copy-start | bytes 6291460
  32.5 1.4 %copy-start.5 = (s32[2,130816]{1,0:T(2,128)S(1)}, s32[2,130816]{1,0:T(2,128)}, u32[]{:S(2)}) copy-start(s32[2,130816]{1,0:T(2,128)} %links_ref.1) | copy-start | bytes 3139588
  33.8 1.5 %copy-start.7 = (bf16[1,1,128,512]{3,2,1,0:T(8,128)(2,1)S(1)}, bf16[1,1,128,512]{3,2,1,0:T(8,128)(2,1)}, u32[]{:S(2)}) copy-start(bf16[1,1,128,512]{3,2,1,0:T(8,128)(2,1)} %param.14) | copy-start | bytes 393220
  33.8 1.5 %copy-start.9 = (bf16[1,1,128,512]{3,2,1,0:T(8,128)(2,1)S(1)}, bf16[1,1,128,512]{3,2,1,0:T(8,128)(2,1)}, u32[]{:S(2)}) copy-start(bf16[1,1,128,512]{3,2,1,0:T(8,128)(2,1)} %param.15) | copy-start | bytes 393220
  35.4 1.6 %copy-start.2 = (bf16[2,2,512,512]{3,2,1,0:T(8,128)(2,1)S(1)}, bf16[2,2,512,512]{3,2,1,0:T(8,128)(2,1)}, u32[]{:S(2)}) copy-start(bf16[2,2,512,512]{3,2,1,0:T(8,128)(2,1)} %constant.34.clone.lead_ref) | copy-start | bytes 6291460
  39.3 1.0 %copy-start.3 = (f32[2,256,512]{2,1,0:T(8,128)}, f32[2,256,512]{2,1,0:T(8,128)S(1)}, u32[]{:S(2)}) copy-start(f32[2,256,512]{2,1,0:T(8,128)S(1)} %get-tuple-element.11.a_ref) | copy-start | bytes 3145732
  59.5 1.2 %copy-start.4 = (f32[2,256,512]{2,1,0:T(8,128)S(1)}, f32[2,256,512]{2,1,0:T(8,128)}, u32[]{:S(2)}) copy-start(f32[2,256,512]{2,1,0:T(8,128)} %copy-done.3) | copy-start | bytes 3145732

commit v2 on v1

--- a/solution.py
+++ b/solution.py
@@ -21,6 +21,7 @@
 VT = 128
 NBLK = 8
 LINK_WINDOW = 256
+X_PIECES = 4
 
 w_chirp = 0.37
 grad_scale = 0.1
@@ -74,16 +75,49 @@
     return np_bf16(np.stack(trailing)), np_bf16(np.stack(leading, axis=1))
 
 
-def contrib_kernel(x_ref, u_ref, v_ref, w_ref, first_ref, turn_ref, last_ref, out_ref, pack_ref, spread, lined, placed):
+def in_hbm(*arrays):
+    return [pltpu.with_memory_space_constraint(one, pltpu.HBM) for one in arrays]
+
+
+def contrib_kernel(
+    x_hbm, u_hbm, v_hbm, w_hbm, first_hbm, turn_hbm, last_hbm,
+    out_ref, pack_ref,
+    x_ref, w_ref, first_ref, turn_ref, last_ref, spread, lined, placed, x_sem, sem,
+):
     rows = x_ref.shape[1]
-    pack_ref[0:VT, :] = u_ref[...]
-    pack_ref[VT : 2 * VT, :] = v_ref[...]
-    pack_ref[2 * VT : 2 * VT + 16, :] = jnp.zeros((16, SG), bf16)
-    pack_ref[2 * VT : 2 * VT + 16, 0:VT] = w_ref[...]
-    for part in range(2):
-        for a in range(32):
-            at = (part * 32 + a) * rows
-            spread[at : at + rows, :] = x_ref[part, :, a * 128 : (a + 1) * 128].astype(f32)
+    chunk = FS // X_PIECES
+    pieces = [
+        pltpu.make_async_copy(
+            x_hbm.at[:, :, pl.ds(c * chunk, chunk)], x_ref.at[:, :, pl.ds(c * chunk, chunk)], x_sem.at[c]
+        )
+        for c in range(X_PIECES)
+    ]
+    others = [
+        pltpu.make_async_copy(source, target, sem.at[i])
+        for i, (source, target) in enumerate(
+            (
+                (first_hbm, first_ref),
+                (turn_hbm, turn_ref),
+                (last_hbm, last_ref),
+                (u_hbm, pack_ref.at[pl.ds(0, VT), :]),
+                (v_hbm, pack_ref.at[pl.ds(VT, VT), :]),
+                (w_hbm, w_ref),
+            )
+        )
+    ]
+    for copy in pieces + others:
+        copy.start()
+    per_piece = 32 // X_PIECES
+    for c in range(X_PIECES):
+        pieces[c].wait()
+        for part in range(2):
+            for a in range(c * per_piece, (c + 1) * per_piece):
+                at = (part * 32 + a) * rows
+                spread[at : at + rows, :] = x_ref[part, :, a * 128 : (a + 1) * 128].astype(f32)
+    for copy in others:
+        copy.wait()
+    weights = jnp.concatenate([w_ref[...].astype(f32), jnp.zeros((16 - NW, VT), f32)], axis=0).astype(bf16)
+    pack_ref[2 * VT : 2 * VT + 16, :] = jnp.concatenate([weights] * (SG // VT), axis=1)
     for m in range(rows):
         lined[:, m * 128 : (m + 1) * 128] = spread[pl.ds(m, 64, stride=rows), :].astype(bf16)
     turn_re = turn_ref[0]
@@ -118,29 +152,50 @@
 def contributions(x, u, v, w):
     rows = x.shape[1]
     first, turn, last = section_tables()
+    anywhere = pl.BlockSpec(memory_space=pl.ANY)
+    vmem = pl.BlockSpec(memory_space=pltpu.VMEM)
     return pl.pallas_call(
         contrib_kernel,
         out_shape=(
-            jax.ShapeDtypeStruct((64, rows, 128), bf16),
-            jax.ShapeDtypeStruct((2 * VT + 16, SG), bf16),
+            pltpu.VMEM((64, rows, 128), bf16),
+            pltpu.VMEM((2 * VT + 16, SG), bf16),
         ),
+        in_specs=[anywhere] * 7,
+        out_specs=(vmem, vmem),
         scratch_shapes=[
+            pltpu.VMEM((2, rows, FS), bf16),
+            pltpu.VMEM((NW, VT), bf16),
+            pltpu.VMEM((64, 64), bf16),
+            pltpu.VMEM((2, 64, 128), f32),
+            pltpu.VMEM((64, 256), bf16),
             pltpu.VMEM((64 * rows, 128), f32),
             pltpu.VMEM((64, 128 * rows), bf16),
             pltpu.VMEM((64 * rows, 128), f32),
+            pltpu.SemaphoreType.DMA((X_PIECES,)),
+            pltpu.SemaphoreType.DMA((6,)),
         ],
         compiler_params=pltpu.CompilerParams(vmem_limit_bytes=16 * MIB),
         cost_estimate=pl.CostEstimate(flops=300_000_000, bytes_accessed=2 * MIB, transcendentals=0),
         name="contrib",
-    )(x, u, v, w, jnp.asarray(first), jnp.asarray(turn), jnp.asarray(last))
-
-
-def taper_kernel(sc_ref, u_ref, v_ref, w_ref, other_ref, trail_ref, lead_ref, b_ref, a_ref):
-    del sc_ref
-    v_all = jnp.concatenate([v_ref[...], other_ref[VT : 2 * VT, :]], axis=0)
-    u_all = jnp.concatenate([u_ref[...], other_ref[0:VT, :]], axis=0)
-    weights = jnp.concatenate([w_ref[...], other_ref[2 * VT : 2 * VT + 16, 0:VT]], axis=1).astype(f32)
+    )(*in_hbm(x, u, v, w, jnp.asarray(first), jnp.asarray(turn), jnp.asarray(last)))
+
+
+def taper_kernel(sc_ref, own_ref, other_ref, trail_hbm, lead_hbm, b_ref, a_ref, trail_ref, lead_ref, sem):
+    trail_copies = [
+        pltpu.make_async_copy(trail_hbm.at[w], trail_ref.at[w], sem.at[w]) for w in range(NW)
+    ]
+    lead_copies = [
+        pltpu.make_async_copy(lead_hbm.at[sc_ref[2], w], lead_ref.at[w], sem.at[NW + w]) for w in range(NW)
+    ]
+    for copy in trail_copies + lead_copies:
+        copy.start()
+    v_all = jnp.concatenate([own_ref[VT : 2 * VT, :], other_ref[VT : 2 * VT, :]], axis=0)
+    u_all = jnp.concatenate([own_ref[0:VT, :], other_ref[0:VT, :]], axis=0)
+    weights = jnp.concatenate(
+        [own_ref[2 * VT : 2 * VT + 16, 0:VT], other_ref[2 * VT : 2 * VT + 16, 0:VT]], axis=1
+    ).astype(f32)
     for w in range(NW):
+        trail_copies[w].wait()
         re_at = slice(w * 256, (w + 1) * 256)
         im_at = slice(512 + w * 256, 512 + (w + 1) * 256)
         for j in range(FGRID):
@@ -148,37 +203,35 @@
             b_ref[j * 128 : (j + 1) * 128, re_at] = got.astype(bf16)
             b_ref[j * 128 : j * 128 + 64, im_at] = (-got[64:128]).astype(bf16)
             b_ref[j * 128 + 64 : (j + 1) * 128, im_at] = got[0:64].astype(bf16)
+    for w in range(NW):
+        lead_copies[w].wait()
+        re_at = slice(w * 256, (w + 1) * 256)
         scale = weights[w : w + 1, :]
-        a_ref[0, :, re_at] = dot_nt(lead_ref[w, 0:256, :], u_all) * scale
-        a_ref[1, :, re_at] = dot_nt(lead_ref[w, 256:512, :], u_all) * scale
-
-
-def taper_transforms(where, u, v, w, other):
+        a_ref[0, :, re_at] = (dot_nt(lead_ref[w, 0:256, :], u_all) * scale).astype(bf16)
+        a_ref[1, :, re_at] = (dot_nt(lead_ref[w, 256:512, :], u_all) * scale).astype(bf16)
+
+
+def taper_transforms(where, own, other):
     trailing, leading = taper_tables()
-    whole = lambda shape: pl.BlockSpec(shape, lambda i, sc: (0,) * len(shape))
+    anywhere = pl.BlockSpec(memory_space=pl.ANY)
+    vmem = pl.BlockSpec(memory_space=pltpu.VMEM)
     return pl.pallas_call(
         taper_kernel,
         out_shape=(
-            jax.ShapeDtypeStruct((2 * SG, 1024), bf16),
-            jax.ShapeDtypeStruct((2, SG // 2, 512), f32),
+            pltpu.VMEM((2 * SG, 1024), bf16),
+            pltpu.VMEM((2, SG // 2, 512), bf16),
         ),
-        grid_spec=pltpu.PrefetchScalarGridSpec(
-            num_scalar_prefetch=1,
-            grid=(1,),
-            in_specs=[
-                whole((VT, SG)),
-                whole((VT, SG)),
-                whole((16, VT)),
-                whole((2 * VT + 16, SG)),
-                whole((NW, 2 * SG, SG)),
-                pl.BlockSpec((None, NW, SG, SG), lambda i, sc: (sc[2], 0, 0, 0)),
-            ],
-            out_specs=(whole((2 * SG, 1024)), whole((2, SG // 2, 512))),
-        ),
+        in_specs=[pl.BlockSpec(memory_space=pltpu.SMEM), vmem, vmem, anywhere, anywhere],
+        out_specs=(vmem, vmem),
+        scratch_shapes=[
+            pltpu.VMEM((NW, 2 * SG, SG), bf16),
+            pltpu.VMEM((NW, SG, SG), bf16),
+            pltpu.SemaphoreType.DMA((2 * NW,)),
+        ],
         compiler_params=pltpu.CompilerParams(vmem_limit_bytes=24 * MIB),
         cost_estimate=pl.CostEstimate(flops=800_000_000, bytes_accessed=8 * MIB, transcendentals=0),
         name="tapers",
-    )(where, u, v, w, other, jnp.asarray(trailing), jnp.asarray(leading))
+    )(where, own, other, *in_hbm(jnp.asarray(trailing), jnp.asarray(leading)))
 
 
 def slots_kernel(sc_ref, table_ref, obs_ref, links_ref, gains_ref, out_ref, window, factors, link_sem, gain_sem):
@@ -203,15 +256,15 @@
     slot = lax.broadcasted_iota(jnp.int32, (1, VT), 1)
     members = []
     chooser = []
-    live = jnp.zeros((1, VT), f32)
+    blocks_of = jnp.full((1, VT), -1.0, f32)
     channels = jnp.zeros((1, VT), f32)
     index = lax.broadcasted_iota(jnp.int32, (LINK_WINDOW, VT), 0)
-    for channel, shift, amount, start in blocks:
+    for b, (channel, shift, amount, start) in enumerate(blocks):
         inside = (slot >= start) & (slot < start + amount)
         member = jnp.where(inside, 1.0, 0.0)
         members.append(member)
-        live = live + member
-        channels = channels + member * channel.astype(f32)
+        blocks_of = jnp.where(inside, float(b), blocks_of)
+        channels = jnp.where(slot == NBLK * sc_ref[2] + (64 + b), channel.astype(f32), channels)
         want = jnp.where(inside, slot - start + shift, -1)
         chooser.append(jnp.where(index == want, 1.0, 0.0).astype(bf16))
     for copy in copies:
@@ -250,8 +303,8 @@
     out_ref[12:16, :] = gain_first
     out_ref[16:20, :] = gain_second
     out_ref[20:22, :] = stations
-    out_ref[22:23, :] = channels
-    out_ref[23:24, :] = live
+    out_ref[22:23, :] = blocks_of
+    out_ref[23:24, :] = channels
 
 
 def slot_rows(where, table, observed, links, gains):
@@ -271,7 +324,7 @@
         compiler_params=pltpu.CompilerParams(vmem_limit_bytes=8 * MIB),
         cost_estimate=pl.CostEstimate(flops=50_000_000, bytes_accessed=2 * MIB, transcendentals=0),
         name="slots",
-    )(where, table, observed, links, gains)
+    )(where, table, observed, *in_hbm(links, gains))
 
 
 def predict_kernel(sc_ref, got_ref, b_ref, a_ref, info_ref, out_ref):
@@ -290,8 +343,8 @@
         at = slice(w * 256, (w + 1) * 256)
         along_re = jnp.dot(left, b_ref[:, w * 256 : (w + 1) * 256], preferred_element_type=f32)
         along_im = jnp.dot(left, b_ref[:, 512 + w * 256 : 512 + (w + 1) * 256], preferred_element_type=f32)
-        a_re = a_ref[0, :, at]
-        a_im = a_ref[1, :, at]
+        a_re = a_ref[0, :, at].astype(f32)
+        a_im = a_ref[1, :, at].astype(f32)
         sum_re = jnp.sum(a_re * along_re - a_im * along_im, axis=0, keepdims=True)
         sum_im = jnp.sum(a_re * along_im + a_im * along_re, axis=0, keepdims=True)
         for side in range(2):
@@ -326,8 +379,9 @@
 def gradient_kernel(sc_ref, got_ref, resid_ref, out_ref):
     owners = 2
     own_class = sc_ref[1] * owners + sc_ref[2]
-    row_id = lax.broadcasted_iota(jnp.int32, (SG, VT), 0)
-    lane_of = lax.broadcasted_iota(jnp.int32, (VT, VT), 0)
+    row_id = lax.broadcasted_iota(jnp.int32, (NST // 8, VT), 0)
+    block_row = lax.broadcasted_iota(jnp.int32, (VT, VT), 0) >> 2
+    channels = got_ref[0, 23:24, :] + got_ref[1, 23:24, :]
     pick = lambda rows, order: jnp.concatenate([rows[i : i + 1] for i in order], axis=0)
     masks = {}
     values = {}
@@ -347,7 +401,8 @@
         pred_im = jnp.concatenate(pred_im, axis=0)
         gain_first = info[12:16]
         gain_second = info[16:20]
-        live = info[23:24]
+        block = info[22:23].astype(jnp.int32)
+        live = jnp.where(block >= 0, 1.0, 0.0)
         first_re = pick(gain_first, (0, 0, 2, 2))
         first_im = pick(gain_first, (1, 1, 3, 3))
         second_re = pick(gain_second, (0, 2, 0, 2))
@@ -389,11 +444,10 @@
                 [r for p in range(NPOL) for r in (resid_re[p : p + 1], resid_im[p : p + 1])], axis=0
             )
         )
-        channel = info[22:23].astype(jnp.int32)
-        chosen = (lane_of >> 2) == (channel & 31)
+        chosen = block_row == jnp.where(block >= 0, NBLK * o + block, -1)
         for side, terms in ((0, leading), (1, trailing)):
             station = info[20 + side : 21 + side].astype(jnp.int32)
-            key = jnp.where((station & 7) == own_class, (station >> 3) * 8 + (channel >> 5), -1)
+            key = jnp.where((station & 7) == own_class, station >> 3, -1)
             masks[side, o] = jnp.where(row_id == key, 1.0, 0.0).astype(bf16)
             tall = jnp.concatenate([terms, terms], axis=0)
             tall = jnp.concatenate([tall] * 16, axis=0)
@@ -401,7 +455,7 @@
     order = [(side, o) for side in range(2) for o in range(owners)]
     mask = jnp.concatenate([masks[at] for at in order], axis=1)
     value = jnp.concatenate([values[at] for at in order], axis=1)
-    out_ref[...] = dot_nt(mask, value).astype(bf16)
+    out_ref[...] = dot_nt(mask, value) + channels
     mine = jnp.where(sc_ref[2] == 0, resid_owner[0], resid_owner[1])
     quarter = resid_ref.shape[3]
     part = mine[:, 0:quarter]
@@ -417,7 +471,7 @@
         gradient_kernel,
         out_shape=(
             jax.ShapeDtypeStruct((1, 2 * NPOL, 1, quarter), f32),
-            jax.ShapeDtypeStruct((SG, 128), bf16),
+            jax.ShapeDtypeStruct((NST // 8, 128), f32),
         ),
         in_specs=[pl.BlockSpec(memory_space=pltpu.SMEM), vmem],
         out_specs=(vmem, vmem),
@@ -425,6 +479,36 @@
         cost_estimate=pl.CostEstimate(flops=70_000_000, bytes_accessed=MIB, transcendentals=0),
         name="gradient",
     )(where, got)
+
+
+def collect_kernel(got_ref, out_ref):
+    turned = got_ref[...].T
+    lanes = turned.shape[1]
+    channel_row = lax.broadcasted_iota(jnp.int32, (128, lanes), 0) >> 2
+    group_row = lax.broadcasted_iota(jnp.int32, (8, lanes), 0)
+    total = jnp.zeros((8, 128), f32)
+    for block in range(2 * NBLK):
+        channel = turned[64 + block : 65 + block].astype(jnp.int32)
+        terms = turned[4 * block : 4 * block + 4]
+        tall = jnp.concatenate([terms, terms], axis=0)
+        tall = jnp.concatenate([tall] * 16, axis=0)
+        value = jnp.where(channel_row == (channel & 31), tall, 0.0).astype(bf16)
+        group = jnp.where(group_row == (channel >> 5), 1.0, 0.0).astype(bf16)
+        total = total + dot_nt(group, value)
+    out_ref[...] = grad_scale * total
+
+
+def collect_rows(got):
+    vmem = pl.BlockSpec(memory_space=pltpu.VMEM)
+    return pl.pallas_call(
+        collect_kernel,
+        out_shape=jax.ShapeDtypeStruct((8, 128), f32),
+        in_specs=[vmem],
+        out_specs=vmem,
+        compiler_params=pltpu.CompilerParams(vmem_limit_bytes=8 * MIB),
+        cost_estimate=pl.CostEstimate(flops=2_000_000, bytes_accessed=65536, transcendentals=0),
+        name="collect",
+    )(got)
 
 
 def on_device(
@@ -441,12 +525,12 @@
     quarter = measured_correlations.shape[3]
     u = taper_leading_axis.reshape(VT, SG)
     v = taper_trailing_axis.reshape(VT, SG)
-    w = jnp.pad(depth_layer_factors.reshape(NW, VT), ((0, 16 - NW), (0, 0)))
+    w = depth_layer_factors.reshape(NW, VT)
     x = tile_spectral_lines.reshape(tile_spectral_lines.shape[2:])
     contrib, pack = contributions(x, u, v, w)
     received = lax.all_to_all(contrib, "facet", split_axis=0, concat_axis=0, tiled=True)
     other = lax.ppermute(pack, "tm", [(0, 1), (1, 0)])
-    b, a = taper_transforms(where, u, v, w, other)
+    b, a = taper_transforms(where, pack, other)
     info = slot_rows(
         where,
         visibility_groups_table.reshape(3, NBLK),
@@ -459,9 +543,9 @@
     gathered = lax.all_to_all(sent, ("pol", "tm"), split_axis=0, concat_axis=0, tiled=True)
     residual, partial_rows = gradient_rows(where, gathered, quarter)
     rows = lax.all_to_all(
-        partial_rows.reshape(64, 8, 128), "facet", split_axis=0, concat_axis=0, tiled=True
+        partial_rows.reshape(NST // 8, 1, 128), "facet", split_axis=0, concat_axis=0, tiled=True
     )
-    gain_grad = grad_scale * jnp.sum(rows.astype(f32), axis=0)
+    gain_grad = collect_rows(rows.reshape(NST // 8, 128))
     return (residual, gain_grad.reshape(1, 4 * NCH))
 
 

time: 99.2 us -> 90.7 us (0.914); the launches traced: 97.3 us -> 90.3 us
  local copies, waits for them, and re-layouts: 11.1 us -> 1.66 us
  Pallas kernels: 10.2 us -> 14.8 us
  blocking collectives: 33.2 us -> 31.6 us
    unnamed x33 -> x9, local copies, waits for them, and re-layouts: 10.3 us -> 1.66 us
    pallas_call x2 -> x3, Pallas kernels: 5.91 us -> 9.97 us  [the longest x1 4.84 us: contributions(): pl.pallas_call(contrib_kernel, out_shape=(pltpu.VMEM((64, rows, 128), bf1...]
    all_to_all x1, blocking collectives: 20.3 us -> 18.8 us  [on_device(): lax.all_to_all(partial_rows.reshape(NST // 8, 1, 128), 'facet', split_axi...]
  transfers between devices with their start and end apart: 2 -> 2, of which waited for: 1 -> 1; matrix products, arithmetic and copies ran while one was open for 0% -> 0% of each run, Pallas kernels for 4% -> 7%
where the time goes in v2:
time: 90.7 us; the launch traced here: 90.3 us
  blocking collectives  31.6 us (35%)
  starting transfers between devices  22.2 us (24%)
  waiting for transfers between devices  19.2 us (21%)
  Pallas kernels  14.8 us (16%)
  local copies, waits for them, and re-layouts  1.66 us (2%)
    all_to_all x1, starting transfers between devices, on_device(): lax.all_to_all(contrib, 'facet', split_axis=0, concat_axis=0, tiled=True)  19.3 us
    all_to_all x1, waiting for transfers between devices, on_device(): lax.all_to_all(contrib, 'facet', split_axis=0, concat_axis=0, tiled=True)  19.2 us
    all_to_all x1, blocking collectives, on_device(): lax.all_to_all(partial_rows.reshape(NST // 8, 1, 128), 'facet', split_axi...  18.8 us
    all_to_all x1, blocking collectives, on_device(): lax.all_to_all(sent, ('pol', 'tm'), split_axis=0, concat_axis=0, tiled=True)  12.8 us
    pallas_call x1, Pallas kernels, contributions(): pl.pallas_call(contrib_kernel, out_shape=(pltpu.VMEM((64, rows, 128), bf1...  4.84 us
    pallas_call x1, Pallas kernels, taper_transforms(): pl.pallas_call(taper_kernel, out_shape=(pltpu.VMEM((2 * SG, 1024), bf16),...  4.06 us
    ppermute x1, starting transfers between devices, on_device(): other = lax.ppermute(pack, 'tm', [(0, 1), (1, 0)])  2.86 us
    pallas_call x1, Pallas kernels, slot_rows(): pl.pallas_call(slots_kernel, out_shape=jax.ShapeDtypeStruct((24, VT), f32...  2.09 us
  transfers between devices with their start and end apart: 2, of which 1 were waited for; matrix products, arithmetic and copies ran while one was open for 0% of the time, Pallas kernels for 7%

profile of v2, /device:TPU:1, one launch (start us, length us, event | category | flops | bytes accessed | tf_op | source)
XLA Modules:
  0.0 90.3 jit_solution(8373166731402263845)
XLA Ops:
  0.6 0.0 copy-start.3
  0.6 0.0 copy-start.2
  0.7 4.8 %contrib.1 = (bf16[64,32,128]{2,1,0:T(8,128)(2,1)}, bf16[272,512]{1,0:T(8,128)(2,1)S(1)}) custom-call(bf16[2,32,4096]{2,1,0:T(8,128)(2,1)} %bitcast.19, bf16[128,512]{1,0:T(8,128)(2,1)} %bitcast.20, bf16[128,512]{1,0:T(8,128)(2,1)} %bitcast.21, bf16[2,128]{1,0:T(2,128)(2,1)} %bitcast.22, bf16[64,64]{1,0:T(8,128)(2,1)} %constant.23.clone.first_hbm, ...), custom_call_target="tpu_custom_call" | custom-call | flops 300000000 | bytes 2097152 | tf_op jit(solution)/shard_map/contrib/pallas_call | solution.py:157
  5.5 19.3 %all-to-all-start = ((bf16[64,32,128]{2,1,0:T(8,128)(2,1)}), bf16[64,32,128]{2,1,0:T(8,128)(2,1)S(1)}, u32[]{:S(2)}, u32[]{:S(2)}) async-start(bf16[64,32,128]{2,1,0:T(8,128)(2,1)} %get-tuple-element.8), calls=%async_computation | async-start | bytes 1048576 | tf_op jit(solution)/shard_map/all_to_all | solution.py:531
  24.8 2.9 %collective-permute-start = (bf16[272,512]{1,0:T(8,128)(2,1)S(1)}, bf16[272,512]{1,0:T(8,128)(2,1)S(1)}, u32[]{:S(2)}, u32[]{:S(2)}) collective-permute-start(bf16[272,512]{1,0:T(8,128)(2,1)S(1)} %get-tuple-element.9.own_ref), channel_id=1, source_target_pairs={{0,1},{1,0},{2,3},{3,2},{4,5},{5,4},{6,7},{7,6},{8,9},{9,8},{10,11... | collective-permute-start | bytes 835592 | tf_op jit(solution)/shard_map/ppermute | solution.py:532
  27.7 0.0 copy-done.3
  27.7 0.1 pad_add_fusion.sc_ref
  27.8 0.0 copy-done.2
  27.8 2.1 %slots.1.info_ref = f32[24,128]{1,0:T(8,128)S(1)} custom-call(s32[3]{0:T(128)S(1)} %pad_add_fusion.sc_ref, s32[3,8]{1,0:T(4,128)S(1)} %bitcast.17, f32[1,8,1,32]{3,2,1,0:T(1,128)S(1)} %copy-done.2, s32[2,130816]{1,0:T(2,128)} %links_ref.1, f32[256,4,512]{2,1,0:T(4,128)} %gains_ref.1), custom_call_target="tpu_custom_call" | custom-call | flops 50000000 | bytes 2097152 | tf_op jit(solution)/shard_map/slots/pallas_call | solution.py:313
  29.9 0.0 collective-permute-done.other_ref
  29.9 0.0 copy-start
  29.9 0.7 copy-done
  30.6 0.0 copy-start.1
  30.6 1.0 %copy-done.1 = bf16[272,512]{1,0:T(8,128)(2,1)S(1)} copy-done((bf16[272,512]{1,0:T(8,128)(2,1)S(1)}, bf16[272,512]{1,0:T(8,128)(2,1)}, u32[]{:S(2)}) %copy-start.1) | copy-done | bytes 278552
  31.5 4.1 %tapers.1 = (bf16[1024,1024]{1,0:T(8,128)(2,1)S(1)}, bf16[2,256,512]{2,1,0:T(8,128)(2,1)S(1)}) custom-call(s32[3]{0:T(128)S(1)} %pad_add_fusion.sc_ref, bf16[272,512]{1,0:T(8,128)(2,1)S(1)} %get-tuple-element.9.own_ref, bf16[272,512]{1,0:T(8,128)(2,1)S(1)} %copy-done.1, bf16[2,1024,512]{2,1,0:T(8,128)(2,1)} %constant.26.clone.trail_hbm, ...), custom_call_target="tpu_custom_call" | custom-call | flops 800000000 | bytes 8388608 | tf_op jit(solution)/shard_map/tapers/pallas_call | solution.py:218
  35.6 19.2 %all-to-all-done.got_ref = bf16[64,32,128]{2,1,0:T(8,128)(2,1)S(1)} async-done(((bf16[64,32,128]{2,1,0:T(8,128)(2,1)}), bf16[64,32,128]{2,1,0:T(8,128)(2,1)S(1)}, u32[]{:S(2)}, u32[]{:S(2)}) %all-to-all-start) | async-done | bytes 524320 | tf_op jit(solution)/shard_map/all_to_all | solution.py:531
  54.8 1.3 %predict.1 = f32[8,24,128]{2,1,0:T(8,128)S(1)} custom-call(s32[3]{0:T(128)S(1)} %pad_add_fusion.sc_ref, bf16[64,32,128]{2,1,0:T(8,128)(2,1)S(1)} %all-to-all-done.got_ref, bf16[1024,1024]{1,0:T(8,128)(2,1)S(1)} %get-tuple-element.10.b_ref, bf16[2,256,512]{2,1,0:T(8,128)(2,1)S(1)} %get-tuple-element.11.a_ref, f32[24,128]{1,0:T(8,128)S(1)} %slots.1.info_ref), custom_call_target="tpu_custom_call" | custom-call | flops 540000000 | bytes 4194304 | tf_op jit(solution)/shard_map/predict/pallas_call | solution.py:368
  56.2 12.8 %all_to_all.15.got_ref = f32[8,24,128]{2,1,0:T(8,128)S(1)} all-to-all(f32[8,24,128]{2,1,0:T(8,128)S(1)} %predict.1), channel_id=1, replica_groups=mesh['facet'=64,'pol'=4,'tm'=2] {'pol','tm'}, dimensions={0} | all-to-all | bytes 196608 | tf_op jit(solution)/shard_map/all_to_all | solution.py:543
  69.0 1.4 %gradient.1 = (f32[1,8,1,32]{3,2,1,0:T(1,128)}, f32[64,128]{1,0:T(8,128)S(1)}) custom-call(s32[3]{0:T(128)S(1)} %pad_add_fusion.sc_ref, f32[8,24,128]{2,1,0:T(8,128)S(1)} %all_to_all.15.got_ref), custom_call_target="tpu_custom_call" | custom-call | flops 70000000 | bytes 1048576 | tf_op jit(solution)/shard_map/gradient/pallas_call | solution.py:470
  70.4 18.8 %all_to_all.16 = f32[64,1,128]{2,1,0:T(1,128)S(1)} all-to-all(f32[64,1,128]{2,1,0:T(1,128)S(1)} %bitcast.16), channel_id=1, replica_groups=mesh['facet'=64,'pol'=4,'tm'=2] {'facet'}, dimensions={0} | all-to-all | bytes 65536 | tf_op jit(solution)/shard_map/all_to_all | solution.py:545
  89.2 1.1 %collect.1 = f32[8,128]{1,0:T(8,128)} custom-call(f32[64,128]{1,0:T(8,128)S(1)} %bitcast.15), custom_call_target="tpu_custom_call" | custom-call | flops 2000000 | bytes 65536 | tf_op jit(solution)/shard_map/collect/pallas_call | solution.py:503
  (1 shorter events, 0.0 us)
Async XLA Ops:
  0.6 27.1 %copy-start.3 = (s32[1,1,3,8]{3,1,2,0:T(1,128)S(1)}, s32[1,1,3,8]{3,1,2,0:T(1,128)}, u32[]{:S(2)}) copy-start(s32[1,1,3,8]{3,1,2,0:T(1,128)} %param.18) | copy-start | bytes 292
  0.6 27.1 %copy-start.2 = (f32[1,8,1,32]{3,2,1,0:T(1,128)S(1)}, f32[1,8,1,32]{3,2,1,0:T(1,128)}, u32[]{:S(2)}) copy-start(f32[1,8,1,32]{3,2,1,0:T(1,128)} %obs_ref.1) | copy-start | bytes 3076
  5.5 49.3 %all-to-all-start = ((bf16[64,32,128]{2,1,0:T(8,128)(2,1)}), bf16[64,32,128]{2,1,0:T(8,128)(2,1)S(1)}, u32[]{:S(2)}, u32[]{:S(2)}) async-start(bf16[64,32,128]{2,1,0:T(8,128)(2,1)} %get-tuple-element.8), calls=%async_computation | async-start | bytes 1048576 | tf_op jit(solution)/shard_map/all_to_all | solution.py:531
  24.8 5.1 %collective-permute-start = (bf16[272,512]{1,0:T(8,128)(2,1)S(1)}, bf16[272,512]{1,0:T(8,128)(2,1)S(1)}, u32[]{:S(2)}, u32[]{:S(2)}) collective-permute-start(bf16[272,512]{1,0:T(8,128)(2,1)S(1)} %get-tuple-element.9.own_ref), channel_id=1, source_target_pairs={{0,1},{1,0},{2,3},{3,2},{4,5},{5,4},{6,7},{7,6},{8,9},{9,8},{10,11... | collective-permute-start | bytes 835592 | tf_op jit(solution)/shard_map/ppermute | solution.py:532
  29.9 0.7 copy-start
  30.6 1.0 %copy-start.1 = (bf16[272,512]{1,0:T(8,128)(2,1)S(1)}, bf16[272,512]{1,0:T(8,128)(2,1)}, u32[]{:S(2)}) copy-start(bf16[272,512]{1,0:T(8,128)(2,1)} %copy-done) | copy-start | bytes 835588

commit v3 on v2

--- a/solution.py
+++ b/solution.py
@@ -21,7 +21,7 @@
 VT = 128
 NBLK = 8
 LINK_WINDOW = 256
-X_PIECES = 4
+BATCHES = 2
 
 w_chirp = 0.37
 grad_scale = 0.1
@@ -81,51 +81,46 @@
 
 def contrib_kernel(
     x_hbm, u_hbm, v_hbm, w_hbm, first_hbm, turn_hbm, last_hbm,
-    out_ref, pack_ref,
-    x_ref, w_ref, first_ref, turn_ref, last_ref, spread, lined, placed, x_sem, sem,
+    out_hbm, pack_ref,
+    x_ref, w_ref, first_ref, turn_ref, last_ref, spread, lined, placed, out_ref, x_sem, sem, out_sem,
 ):
     rows = x_ref.shape[1]
-    chunk = FS // X_PIECES
+    batch = rows // BATCHES
     pieces = [
         pltpu.make_async_copy(
-            x_hbm.at[:, :, pl.ds(c * chunk, chunk)], x_ref.at[:, :, pl.ds(c * chunk, chunk)], x_sem.at[c]
+            x_hbm.at[:, pl.ds(h * batch, batch), :], x_ref.at[:, pl.ds(h * batch, batch), :], x_sem.at[h]
         )
-        for c in range(X_PIECES)
+        for h in range(BATCHES)
     ]
-    others = [
+    tables = [
         pltpu.make_async_copy(source, target, sem.at[i])
         for i, (source, target) in enumerate(
+            ((first_hbm, first_ref), (turn_hbm, turn_ref), (last_hbm, last_ref))
+        )
+    ]
+    tapers = [
+        pltpu.make_async_copy(source, target, sem.at[3 + i])
+        for i, (source, target) in enumerate(
             (
-                (first_hbm, first_ref),
-                (turn_hbm, turn_ref),
-                (last_hbm, last_ref),
+                (w_hbm, w_ref),
                 (u_hbm, pack_ref.at[pl.ds(0, VT), :]),
                 (v_hbm, pack_ref.at[pl.ds(VT, VT), :]),
-                (w_hbm, w_ref),
             )
         )
     ]
-    for copy in pieces + others:
+    results = [
+        pltpu.make_async_copy(out_ref.at[h], out_hbm.at[:, pl.ds(h * batch, batch), :], out_sem.at[h])
+        for h in range(BATCHES)
+    ]
+    for copy in pieces[:1] + tables + pieces[1:] + tapers:
         copy.start()
-    per_piece = 32 // X_PIECES
-    for c in range(X_PIECES):
-        pieces[c].wait()
-        for part in range(2):
-            for a in range(c * per_piece, (c + 1) * per_piece):
-                at = (part * 32 + a) * rows
-                spread[at : at + rows, :] = x_ref[part, :, a * 128 : (a + 1) * 128].astype(f32)
-    for copy in others:
-        copy.wait()
-    weights = jnp.concatenate([w_ref[...].astype(f32), jnp.zeros((16 - NW, VT), f32)], axis=0).astype(bf16)
-    pack_ref[2 * VT : 2 * VT + 16, :] = jnp.concatenate([weights] * (SG // VT), axis=1)
-    for m in range(rows):
-        lined[:, m * 128 : (m + 1) * 128] = spread[pl.ds(m, 64, stride=rows), :].astype(bf16)
-    turn_re = turn_ref[0]
-    turn_im = turn_ref[1]
-    for pair in range(rows // 2):
-        section = jnp.dot(
-            first_ref[...], lined[:, pair * 256 : (pair + 1) * 256], preferred_element_type=f32
-        )
+
+    def section_of(pair):
+        return jnp.dot(first_ref[...], lined[:, pair * 256 : (pair + 1) * 256], preferred_element_type=f32)
+
+    def turned_of(section):
+        turn_re = turn_ref[0]
+        turn_im = turn_ref[1]
         sides = []
         for half in range(2):
             one = section[:, half * 128 : (half + 1) * 128]
@@ -142,11 +137,54 @@
                     axis=0,
                 )
             )
-        result = dot_nt(last_ref[...], jnp.concatenate(sides, axis=0))
+        return jnp.concatenate(sides, axis=0)
+
+    def finish(pair, turned):
+        result = dot_nt(last_ref[...], turned)
         placed[pl.ds(2 * pair, 64, stride=rows), :] = result[:, 0:128]
         placed[pl.ds(2 * pair + 1, 64, stride=rows), :] = result[:, 128:256]
-    for s in range(64):
-        out_ref[s] = placed[s * rows : (s + 1) * rows, :].astype(bf16)
+
+    def line_up(h):
+        pieces[h].wait()
+        for part in range(2):
+            for a in range(32):
+                at = (part * 32 + a) * rows + h * batch
+                spread[at : at + batch, :] = x_ref[
+                    part, h * batch : (h + 1) * batch, a * 128 : (a + 1) * 128
+                ].astype(f32)
+        for m in range(h * batch, (h + 1) * batch):
+            lined[:, m * 128 : (m + 1) * 128] = spread[pl.ds(m, 64, stride=rows), :].astype(bf16)
+
+    def send(h):
+        for s in range(64):
+            at = s * rows + h * batch
+            out_ref[h, s] = placed[at : at + batch, :].astype(bf16)
+        results[h].start()
+
+    per = batch // 2
+    line_up(0)
+    for copy in tables:
+        copy.wait()
+    pairs = rows // 2
+    sections = {0: section_of(0), 1: section_of(1)}
+    turned = {}
+    for step in range(pairs + 1):
+        if step + 2 < pairs:
+            if (step + 2) % per == 0:
+                line_up((step + 2) // per)
+            sections[step + 2] = section_of(step + 2)
+        if step < pairs:
+            turned[step] = turned_of(sections.pop(step))
+        if step >= 1:
+            finish(step - 1, turned.pop(step - 1))
+            if step % per == 0:
+                send(step // per - 1)
+    for copy in tapers:
+        copy.wait()
+    weights = jnp.concatenate([w_ref[...].astype(f32), jnp.zeros((16 - NW, VT), f32)], axis=0).astype(bf16)
+    pack_ref[2 * VT : 2 * VT + 16, :] = jnp.concatenate([weights] * (SG // VT), axis=1)
+    for copy in results:
+        copy.wait()
 
 
 def contributions(x, u, v, w):
@@ -157,11 +195,11 @@
     return pl.pallas_call(
         contrib_kernel,
         out_shape=(
-            pltpu.VMEM((64, rows, 128), bf16),
+            jax.ShapeDtypeStruct((64, rows, 128), bf16),
             pltpu.VMEM((2 * VT + 16, SG), bf16),
         ),
         in_specs=[anywhere] * 7,
-        out_specs=(vmem, vmem),
+        out_specs=(anywhere, vmem),
         scratch_shapes=[
             pltpu.VMEM((2, rows, FS), bf16),
             pltpu.VMEM((NW, VT), bf16),
@@ -171,8 +209,10 @@
             pltpu.VMEM((64 * rows, 128), f32),
             pltpu.VMEM((64, 128 * rows), bf16),
             pltpu.VMEM((64 * rows, 128), f32),
-            pltpu.SemaphoreType.DMA((X_PIECES,)),
+            pltpu.VMEM((BATCHES, 64, rows // BATCHES, 128), bf16),
+            pltpu.SemaphoreType.DMA((BATCHES,)),
             pltpu.SemaphoreType.DMA((6,)),
+            pltpu.SemaphoreType.DMA((BATCHES,)),
         ],
         compiler_params=pltpu.CompilerParams(vmem_limit_bytes=16 * MIB),
         cost_estimate=pl.CostEstimate(flops=300_000_000, bytes_accessed=2 * MIB, transcendentals=0),
@@ -457,21 +497,16 @@
     value = jnp.concatenate([values[at] for at in order], axis=1)
     out_ref[...] = dot_nt(mask, value) + channels
     mine = jnp.where(sc_ref[2] == 0, resid_owner[0], resid_owner[1])
-    quarter = resid_ref.shape[3]
-    part = mine[:, 0:quarter]
-    for q in range(1, NPOL):
-        part = jnp.where(sc_ref[1] == q, mine[:, q * quarter : (q + 1) * quarter], part)
-    for row in range(2 * NPOL):
-        resid_ref[0, row] = part[row : row + 1, :]
-
-
-def gradient_rows(where, got, quarter):
+    resid_ref[...] = mine
+
+
+def gradient_rows(where, got):
     vmem = pl.BlockSpec(memory_space=pltpu.VMEM)
     return pl.pallas_call(
         gradient_kernel,
         out_shape=(
-            jax.ShapeDtypeStruct((1, 2 * NPOL, 1, quarter), f32),
-            jax.ShapeDtypeStruct((NST // 8, 128), f32),
+            pltpu.VMEM((2 * NPOL, VT), f32),
+            pltpu.VMEM((NST // 8, 128), f32),
         ),
         in_specs=[pl.BlockSpec(memory_space=pltpu.SMEM), vmem],
         out_specs=(vmem, vmem),
@@ -481,12 +516,22 @@
     )(where, got)
 
 
-def collect_kernel(got_ref, out_ref):
+def collect_kernel(sc_ref, got_ref, mine_ref, out_hbm, resid_hbm, out_ref, resid_ref, sem):
+    mine = mine_ref[...]
+    quarter = resid_ref.shape[3]
+    part = mine[:, 0:quarter]
+    for q in range(1, NPOL):
+        part = jnp.where(sc_ref[1] == q, mine[:, q * quarter : (q + 1) * quarter], part)
+    for row in range(2 * NPOL):
+        resid_ref[0, row] = part[row : row + 1, :]
+    resid_copy = pltpu.make_async_copy(resid_ref, resid_hbm, sem.at[0])
+    resid_copy.start()
     turned = got_ref[...].T
     lanes = turned.shape[1]
     channel_row = lax.broadcasted_iota(jnp.int32, (128, lanes), 0) >> 2
     group_row = lax.broadcasted_iota(jnp.int32, (8, lanes), 0)
-    total = jnp.zeros((8, 128), f32)
+    values = []
+    groups = []
     for block in range(2 * NBLK):
         channel = turned[64 + block : 65 + block].astype(jnp.int32)
         terms = turned[4 * block : 4 * block + 4]
@@ -494,21 +539,35 @@
         tall = jnp.concatenate([tall] * 16, axis=0)
         value = jnp.where(channel_row == (channel & 31), tall, 0.0).astype(bf16)
         group = jnp.where(group_row == (channel >> 5), 1.0, 0.0).astype(bf16)
-        total = total + dot_nt(group, value)
+        values.append(value)
+        groups.append(group)
+    total = dot_nt(jnp.concatenate(groups, axis=1), jnp.concatenate(values, axis=1))
     out_ref[...] = grad_scale * total
-
-
-def collect_rows(got):
+    out_copy = pltpu.make_async_copy(out_ref, out_hbm, sem.at[1])
+    out_copy.start()
+    out_copy.wait()
+    resid_copy.wait()
+
+
+def collect_rows(where, got, mine, quarter):
     vmem = pl.BlockSpec(memory_space=pltpu.VMEM)
     return pl.pallas_call(
         collect_kernel,
-        out_shape=jax.ShapeDtypeStruct((8, 128), f32),
-        in_specs=[vmem],
-        out_specs=vmem,
+        out_shape=(
+            jax.ShapeDtypeStruct((8, 128), f32),
+            jax.ShapeDtypeStruct((1, 2 * NPOL, 1, quarter), f32),
+        ),
+        in_specs=[pl.BlockSpec(memory_space=pltpu.SMEM), vmem, vmem],
+        out_specs=(pl.BlockSpec(memory_space=pl.ANY),) * 2,
+        scratch_shapes=[
+            pltpu.VMEM((8, 128), f32),
+            pltpu.VMEM((1, 2 * NPOL, 1, quarter), f32),
+            pltpu.SemaphoreType.DMA((2,)),
+        ],
         compiler_params=pltpu.CompilerParams(vmem_limit_bytes=8 * MIB),
         cost_estimate=pl.CostEstimate(flops=2_000_000, bytes_accessed=65536, transcendentals=0),
         name="collect",
-    )(got)
+    )(where, got, mine)
 
 
 def on_device(
@@ -541,11 +600,11 @@
     peers = lax.axis_size(("pol", "tm"))
     sent = partial_predictions(where, received, b, a, info, peers)
     gathered = lax.all_to_all(sent, ("pol", "tm"), split_axis=0, concat_axis=0, tiled=True)
-    residual, partial_rows = gradient_rows(where, gathered, quarter)
+    mine, partial_rows = gradient_rows(where, gathered)
     rows = lax.all_to_all(
         partial_rows.reshape(NST // 8, 1, 128), "facet", split_axis=0, concat_axis=0, tiled=True
     )
-    gain_grad = collect_rows(rows.reshape(NST // 8, 128))
+    gain_grad, residual = collect_rows(where, rows.reshape(NST // 8, 128), mine, quarter)
     return (residual, gain_grad.reshape(1, 4 * NCH))
 
 

time: 90.7 us -> 89.6 us (0.988)
  Pallas kernels: 14.8 us -> 13.7 us
    pallas_call x3, Pallas kernels: 7.35 us -> 6.26 us  [the longest x1 3.95 us: contributions(): pl.pallas_call(contrib_kernel, out_shape=(jax.ShapeDtypeStruct((64, rows,...]
where the time goes in v3:
time: 89.6 us; the launch traced here: 89.2 us
  blocking collectives  31.6 us (35%)
  starting transfers between devices  22.2 us (25%)
  waiting for transfers between devices  19.2 us (21%)
  Pallas kernels  13.7 us (15%)
  local copies, waits for them, and re-layouts  1.67 us (2%)
    all_to_all x1, starting transfers between devices, on_device(): lax.all_to_all(contrib, 'facet', split_axis=0, concat_axis=0, tiled=True)  19.3 us
    all_to_all x1, waiting for transfers between devices, on_device(): lax.all_to_all(contrib, 'facet', split_axis=0, concat_axis=0, tiled=True)  19.2 us
    all_to_all x1, blocking collectives, on_device(): lax.all_to_all(partial_rows.reshape(NST // 8, 1, 128), 'facet', split_axi...  18.8 us
    all_to_all x1, blocking collectives, on_device(): lax.all_to_all(sent, ('pol', 'tm'), split_axis=0, concat_axis=0, tiled=True)  12.8 us
    pallas_call x1, Pallas kernels, taper_transforms(): pl.pallas_call(taper_kernel, out_shape=(pltpu.VMEM((2 * SG, 1024), bf16),...  4.06 us
    pallas_call x1, Pallas kernels, contributions(): pl.pallas_call(contrib_kernel, out_shape=(jax.ShapeDtypeStruct((64, rows,...  3.95 us
    ppermute x1, starting transfers between devices, on_device(): other = lax.ppermute(pack, 'tm', [(0, 1), (1, 0)])  2.86 us
    pallas_call x1, Pallas kernels, slot_rows(): pl.pallas_call(slots_kernel, out_shape=jax.ShapeDtypeStruct((24, VT), f32...  2.09 us
  transfers between devices with their start and end apart: 2, of which 1 were waited for; matrix products, arithmetic and copies ran while one was open for 0% of the time, Pallas kernels for 7%

profile of v3, /device:TPU:1, one launch (start us, length us, event | category | flops | bytes accessed | tf_op | source)
XLA Modules:
  0.0 89.2 jit_solution(9183830299582357058)
XLA Ops:
  0.6 0.0 copy-start.3
  0.6 0.0 copy-start.2
  0.7 3.9 %contrib.1 = (bf16[64,32,128]{2,1,0:T(8,128)(2,1)}, bf16[272,512]{1,0:T(8,128)(2,1)S(1)}) custom-call(bf16[2,32,4096]{2,1,0:T(8,128)(2,1)} %bitcast.18, bf16[128,512]{1,0:T(8,128)(2,1)} %bitcast.19, bf16[128,512]{1,0:T(8,128)(2,1)} %bitcast.20, bf16[2,128]{1,0:T(2,128)(2,1)} %bitcast.22, bf16[64,64]{1,0:T(8,128)(2,1)} %constant.23.clone.first_hbm, ...), custom_call_target="tpu_custom_call" | custom-call | flops 300000000 | bytes 2097152 | tf_op jit(solution)/shard_map/contrib/pallas_call | solution.py:195
  4.6 19.3 %all-to-all-start = ((bf16[64,32,128]{2,1,0:T(8,128)(2,1)}), bf16[64,32,128]{2,1,0:T(8,128)(2,1)S(1)}, u32[]{:S(2)}, u32[]{:S(2)}) async-start(bf16[64,32,128]{2,1,0:T(8,128)(2,1)} %get-tuple-element.10), calls=%async_computation | async-start | bytes 1048576 | tf_op jit(solution)/shard_map/all_to_all | solution.py:590
  23.9 2.9 %collective-permute-start = (bf16[272,512]{1,0:T(8,128)(2,1)S(1)}, bf16[272,512]{1,0:T(8,128)(2,1)S(1)}, u32[]{:S(2)}, u32[]{:S(2)}) collective-permute-start(bf16[272,512]{1,0:T(8,128)(2,1)S(1)} %get-tuple-element.11.own_ref), channel_id=1, source_target_pairs={{0,1},{1,0},{2,3},{3,2},{4,5},{5,4},{6,7},{7,6},{8,9},{9,8},{10,11... | collective-permute-start | bytes 835592 | tf_op jit(solution)/shard_map/ppermute | solution.py:591
  26.8 0.0 copy-done.3
  26.8 0.1 pad_add_fusion.sc_ref
  26.9 0.0 copy-done.2
  26.9 2.1 %slots.1.info_ref = f32[24,128]{1,0:T(8,128)S(1)} custom-call(s32[3]{0:T(128)S(1)} %pad_add_fusion.sc_ref, s32[3,8]{1,0:T(4,128)S(1)} %bitcast.17, f32[1,8,1,32]{3,2,1,0:T(1,128)S(1)} %copy-done.2, s32[2,130816]{1,0:T(2,128)} %links_ref.1, f32[256,4,512]{2,1,0:T(4,128)} %gains_ref.1), custom_call_target="tpu_custom_call" | custom-call | flops 50000000 | bytes 2097152 | tf_op jit(solution)/shard_map/slots/pallas_call | solution.py:353
  29.0 0.0 collective-permute-done.other_ref
  29.0 0.0 copy-start
  29.0 0.7 copy-done
  29.7 0.0 copy-start.1
  29.7 1.0 %copy-done.1 = bf16[272,512]{1,0:T(8,128)(2,1)S(1)} copy-done((bf16[272,512]{1,0:T(8,128)(2,1)S(1)}, bf16[272,512]{1,0:T(8,128)(2,1)}, u32[]{:S(2)}) %copy-start.1) | copy-done | bytes 278552
  30.7 4.1 %tapers.1 = (bf16[1024,1024]{1,0:T(8,128)(2,1)S(1)}, bf16[2,256,512]{2,1,0:T(8,128)(2,1)S(1)}) custom-call(s32[3]{0:T(128)S(1)} %pad_add_fusion.sc_ref, bf16[272,512]{1,0:T(8,128)(2,1)S(1)} %get-tuple-element.11.own_ref, bf16[272,512]{1,0:T(8,128)(2,1)S(1)} %copy-done.1, bf16[2,1024,512]{2,1,0:T(8,128)(2,1)} %constant.26.clone.trail_hbm, ...), custom_call_target="tpu_custom_call" | custom-call | flops 800000000 | bytes 8388608 | tf_op jit(solution)/shard_map/tapers/pallas_call | solution.py:258
  34.7 19.2 %all-to-all-done.got_ref = bf16[64,32,128]{2,1,0:T(8,128)(2,1)S(1)} async-done(((bf16[64,32,128]{2,1,0:T(8,128)(2,1)}), bf16[64,32,128]{2,1,0:T(8,128)(2,1)S(1)}, u32[]{:S(2)}, u32[]{:S(2)}) %all-to-all-start) | async-done | bytes 524320 | tf_op jit(solution)/shard_map/all_to_all | solution.py:590
  53.9 1.3 %predict.1 = f32[8,24,128]{2,1,0:T(8,128)S(1)} custom-call(s32[3]{0:T(128)S(1)} %pad_add_fusion.sc_ref, bf16[64,32,128]{2,1,0:T(8,128)(2,1)S(1)} %all-to-all-done.got_ref, bf16[1024,1024]{1,0:T(8,128)(2,1)S(1)} %get-tuple-element.12.b_ref, bf16[2,256,512]{2,1,0:T(8,128)(2,1)S(1)} %get-tuple-element.13.a_ref, f32[24,128]{1,0:T(8,128)S(1)} %slots.1.info_ref), custom_call_target="tpu_custom_call" | custom-call | flops 540000000 | bytes 4194304 | tf_op jit(solution)/shard_map/predict/pallas_call | solution.py:408
  55.3 12.8 %all_to_all.15.got_ref = f32[8,24,128]{2,1,0:T(8,128)S(1)} all-to-all(f32[8,24,128]{2,1,0:T(8,128)S(1)} %predict.1), channel_id=1, replica_groups=mesh['facet'=64,'pol'=4,'tm'=2] {'pol','tm'}, dimensions={0} | all-to-all | bytes 196608 | tf_op jit(solution)/shard_map/all_to_all | solution.py:602
  68.1 0.7 gradient.1
  68.8 18.8 %all_to_all.16 = f32[64,1,128]{2,1,0:T(1,128)S(1)} all-to-all(f32[64,1,128]{2,1,0:T(1,128)S(1)} %bitcast.16), channel_id=1, replica_groups=mesh['facet'=64,'pol'=4,'tm'=2] {'facet'}, dimensions={0} | all-to-all | bytes 65536 | tf_op jit(solution)/shard_map/all_to_all | solution.py:604
  87.6 1.6 %collect.1 = (f32[8,128]{1,0:T(8,128)}, f32[1,8,1,32]{3,2,1,0:T(1,128)}) custom-call(s32[3]{0:T(128)S(1)} %pad_add_fusion.sc_ref, f32[64,128]{1,0:T(8,128)S(1)} %bitcast.15, f32[8,128]{1,0:T(8,128)S(1)} %get-tuple-element.15.mine_ref), custom_call_target="tpu_custom_call" | custom-call | flops 2000000 | bytes 65536 | tf_op jit(solution)/shard_map/collect/pallas_call | solution.py:554
  (1 shorter events, 0.0 us)
Async XLA Ops:
  0.6 26.2 %copy-start.3 = (s32[1,1,3,8]{3,1,2,0:T(1,128)S(1)}, s32[1,1,3,8]{3,1,2,0:T(1,128)}, u32[]{:S(2)}) copy-start(s32[1,1,3,8]{3,1,2,0:T(1,128)} %param.18) | copy-start | bytes 292
  0.6 26.2 %copy-start.2 = (f32[1,8,1,32]{3,2,1,0:T(1,128)S(1)}, f32[1,8,1,32]{3,2,1,0:T(1,128)}, u32[]{:S(2)}) copy-start(f32[1,8,1,32]{3,2,1,0:T(1,128)} %obs_ref.1) | copy-start | bytes 3076
  4.6 49.3 %all-to-all-start = ((bf16[64,32,128]{2,1,0:T(8,128)(2,1)}), bf16[64,32,128]{2,1,0:T(8,128)(2,1)S(1)}, u32[]{:S(2)}, u32[]{:S(2)}) async-start(bf16[64,32,128]{2,1,0:T(8,128)(2,1)} %get-tuple-element.10), calls=%async_computation | async-start | bytes 1048576 | tf_op jit(solution)/shard_map/all_to_all | solution.py:590
  23.9 5.1 %collective-permute-start = (bf16[272,512]{1,0:T(8,128)(2,1)S(1)}, bf16[272,512]{1,0:T(8,128)(2,1)S(1)}, u32[]{:S(2)}, u32[]{:S(2)}) collective-permute-start(bf16[272,512]{1,0:T(8,128)(2,1)S(1)} %get-tuple-element.11.own_ref), channel_id=1, source_target_pairs={{0,1},{1,0},{2,3},{3,2},{4,5},{5,4},{6,7},{7,6},{8,9},{9,8},{10,11... | collective-permute-start | bytes 835592 | tf_op jit(solution)/shard_map/ppermute | solution.py:591
  29.0 0.7 copy-start
  29.7 1.0 %copy-start.1 = (bf16[272,512]{1,0:T(8,128)(2,1)S(1)}, bf16[272,512]{1,0:T(8,128)(2,1)}, u32[]{:S(2)}) copy-start(bf16[272,512]{1,0:T(8,128)(2,1)} %copy-done) | copy-start | bytes 835588

commit v4 on v3

--- a/solution.py
+++ b/solution.py
@@ -335,7 +335,9 @@
     quarter = obs_ref.shape[3]
     lane = lax.broadcasted_iota(jnp.int32, (1, VT), 1)
     mine = (lane // quarter) == sc_ref[1]
-    out_ref[0:4, :] = jnp.zeros((4, VT), f32)
+    out_ref[0:1, :] = jnp.full((1, VT), sc_ref[2].astype(f32))
+    out_ref[1:2, :] = jnp.full((1, VT), sc_ref[1].astype(f32))
+    out_ref[2:4, :] = jnp.zeros((2, VT), f32)
     for row in range(2 * NPOL):
         one = obs_ref[0, row]
         spread = jnp.concatenate([one] * (VT // quarter), axis=1)
@@ -367,7 +369,7 @@
     )(where, table, observed, *in_hbm(links, gains))
 
 
-def predict_kernel(sc_ref, got_ref, b_ref, a_ref, info_ref, out_ref):
+def predict_kernel(got_ref, b_ref, a_ref, info_ref, out_ref):
     rows = got_ref.shape[1]
     left = jnp.concatenate(
         [
@@ -390,7 +392,7 @@
         for side in range(2):
             total_re[side] = total_re[side] + sum_re[:, side * VT : (side + 1) * VT]
             total_im[side] = total_im[side] + sum_im[:, side * VT : (side + 1) * VT]
-    first = sc_ref[2] == 0
+    first = info_ref[0:1, :] == 0.0
     rows_out = [
         jnp.where(first, total_re[0], total_re[1]),
         jnp.where(first, total_re[1], total_re[0]),
@@ -403,22 +405,24 @@
         out_ref[to, 8:24, :] = info_ref[8:24, :]
 
 
-def partial_predictions(where, got, b, a, info, peers):
+def partial_predictions(got, b, a, info, peers):
     vmem = pl.BlockSpec(memory_space=pltpu.VMEM)
     return pl.pallas_call(
         predict_kernel,
         out_shape=jax.ShapeDtypeStruct((peers, 24, VT), f32),
-        in_specs=[pl.BlockSpec(memory_space=pltpu.SMEM), vmem, vmem, vmem, vmem],
+        in_specs=[vmem] * 4,
         out_specs=vmem,
         compiler_params=pltpu.CompilerParams(vmem_limit_bytes=20 * MIB),
         cost_estimate=pl.CostEstimate(flops=540_000_000, bytes_accessed=4 * MIB, transcendentals=0),
         name="predict",
-    )(where, got, b, a, info)
-
-
-def gradient_kernel(sc_ref, got_ref, resid_ref, out_ref):
+    )(got, b, a, info)
+
+
+def gradient_kernel(info_ref, got_ref, resid_ref, out_ref):
     owners = 2
-    own_class = sc_ref[1] * owners + sc_ref[2]
+    own_tm = info_ref[0:1, :]
+    own_pol = info_ref[1:2, :]
+    own_class = (own_pol * owners + own_tm).astype(jnp.int32)
     row_id = lax.broadcasted_iota(jnp.int32, (NST // 8, VT), 0)
     block_row = lax.broadcasted_iota(jnp.int32, (VT, VT), 0) >> 2
     channels = got_ref[0, 23:24, :] + got_ref[1, 23:24, :]
@@ -496,32 +500,32 @@
     mask = jnp.concatenate([masks[at] for at in order], axis=1)
     value = jnp.concatenate([values[at] for at in order], axis=1)
     out_ref[...] = dot_nt(mask, value) + channels
-    mine = jnp.where(sc_ref[2] == 0, resid_owner[0], resid_owner[1])
-    resid_ref[...] = mine
-
-
-def gradient_rows(where, got):
+    mine = jnp.where(own_tm == 0.0, resid_owner[0], resid_owner[1])
+    quarter = resid_ref.shape[1]
+    part = mine[:, 0:quarter]
+    for q in range(1, NPOL):
+        part = jnp.where(own_pol[:, 0:quarter] == float(q), mine[:, q * quarter : (q + 1) * quarter], part)
+    resid_ref[...] = part
+
+
+def gradient_rows(info, got):
     vmem = pl.BlockSpec(memory_space=pltpu.VMEM)
     return pl.pallas_call(
         gradient_kernel,
         out_shape=(
-            pltpu.VMEM((2 * NPOL, VT), f32),
+            pltpu.VMEM((2 * NPOL, VT // NPOL), f32),
             pltpu.VMEM((NST // 8, 128), f32),
         ),
-        in_specs=[pl.BlockSpec(memory_space=pltpu.SMEM), vmem],
+        in_specs=[vmem, vmem],
         out_specs=(vmem, vmem),
         compiler_params=pltpu.CompilerParams(vmem_limit_bytes=12 * MIB),
         cost_estimate=pl.CostEstimate(flops=70_000_000, bytes_accessed=MIB, transcendentals=0),
         name="gradient",
-    )(where, got)
-
-
-def collect_kernel(sc_ref, got_ref, mine_ref, out_hbm, resid_hbm, out_ref, resid_ref, sem):
-    mine = mine_ref[...]
-    quarter = resid_ref.shape[3]
-    part = mine[:, 0:quarter]
-    for q in range(1, NPOL):
-        part = jnp.where(sc_ref[1] == q, mine[:, q * quarter : (q + 1) * quarter], part)
+    )(info, got)
+
+
+def collect_kernel(got_ref, mine_ref, out_hbm, resid_hbm, out_ref, resid_ref, sem):
+    part = mine_ref[...]
     for row in range(2 * NPOL):
         resid_ref[0, row] = part[row : row + 1, :]
     resid_copy = pltpu.make_async_copy(resid_ref, resid_hbm, sem.at[0])
@@ -549,7 +553,7 @@
     resid_copy.wait()
 
 
-def collect_rows(where, got, mine, quarter):
+def collect_rows(got, mine, quarter):
     vmem = pl.BlockSpec(memory_space=pltpu.VMEM)
     return pl.pallas_call(
         collect_kernel,
@@ -557,7 +561,7 @@
             jax.ShapeDtypeStruct((8, 128), f32),
             jax.ShapeDtypeStruct((1, 2 * NPOL, 1, quarter), f32),
         ),
-        in_specs=[pl.BlockSpec(memory_space=pltpu.SMEM), vmem, vmem],
+        in_specs=[vmem, vmem],
         out_specs=(pl.BlockSpec(memory_space=pl.ANY),) * 2,
         scratch_shapes=[
             pltpu.VMEM((8, 128), f32),
@@ -567,7 +571,7 @@
         compiler_params=pltpu.CompilerParams(vmem_limit_bytes=8 * MIB),
         cost_estimate=pl.CostEstimate(flops=2_000_000, bytes_accessed=65536, transcendentals=0),
         name="collect",
-    )(where, got, mine)
+    )(got, mine)
 
 
 def on_device(
@@ -598,13 +602,13 @@
         complex_receiver_factors,
     )
     peers = lax.axis_size(("pol", "tm"))
-    sent = partial_predictions(where, received, b, a, info, peers)
+    sent = partial_predictions(received, b, a, info, peers)
     gathered = lax.all_to_all(sent, ("pol", "tm"), split_axis=0, concat_axis=0, tiled=True)
-    mine, partial_rows = gradient_rows(where, gathered)
+    mine, partial_rows = gradient_rows(info, gathered)
     rows = lax.all_to_all(
         partial_rows.reshape(NST // 8, 1, 128), "facet", split_axis=0, concat_axis=0, tiled=True
     )
-    gain_grad, residual = collect_rows(where, rows.reshape(NST // 8, 128), mine, quarter)
+    gain_grad, residual = collect_rows(rows.reshape(NST // 8, 128), mine, quarter)
     return (residual, gain_grad.reshape(1, 4 * NCH))
 
 

time: 89.6 us -> 87.9 us (0.981)
  Pallas kernels: 13.7 us -> 12.1 us
where the time goes in v4:
time: 87.9 us; the launch traced here: 87.6 us
  blocking collectives  31.6 us (36%)
  starting transfers between devices  22.2 us (25%)
  waiting for transfers between devices  19.2 us (22%)
  Pallas kernels  12.1 us (14%)
  local copies, waits for them, and re-layouts  1.67 us (2%)
    all_to_all x1, starting transfers between devices, on_device(): lax.all_to_all(contrib, 'facet', split_axis=0, concat_axis=0, tiled=True)  19.3 us
    all_to_all x1, waiting for transfers between devices, on_device(): lax.all_to_all(contrib, 'facet', split_axis=0, concat_axis=0, tiled=True)  19.2 us
    all_to_all x1, blocking collectives, on_device(): lax.all_to_all(partial_rows.reshape(NST // 8, 1, 128), 'facet', split_axi...  18.8 us
    all_to_all x1, blocking collectives, on_device(): lax.all_to_all(sent, ('pol', 'tm'), split_axis=0, concat_axis=0, tiled=True)  12.8 us
    pallas_call x1, Pallas kernels, taper_transforms(): pl.pallas_call(taper_kernel, out_shape=(pltpu.VMEM((2 * SG, 1024), bf16),...  4.06 us
    pallas_call x1, Pallas kernels, contributions(): pl.pallas_call(contrib_kernel, out_shape=(jax.ShapeDtypeStruct((64, rows,...  3.95 us
    ppermute x1, starting transfers between devices, on_device(): other = lax.ppermute(pack, 'tm', [(0, 1), (1, 0)])  2.86 us
    pallas_call x1, Pallas kernels, slot_rows(): pl.pallas_call(slots_kernel, out_shape=jax.ShapeDtypeStruct((24, VT), f32...  2.09 us
  transfers between devices with their start and end apart: 2, of which 1 were waited for; matrix products, arithmetic and copies ran while one was open for 0% of the time, Pallas kernels for 7%

profile of v4, /device:TPU:1, one launch (start us, length us, event | category | flops | bytes accessed | tf_op | source)
XLA Modules:
  0.0 87.6 jit_solution(15507304832807528216)
XLA Ops:
  0.6 0.0 copy-start.3
  0.6 0.0 copy-start.2
  0.7 3.9 %contrib.1 = (bf16[64,32,128]{2,1,0:T(8,128)(2,1)}, bf16[272,512]{1,0:T(8,128)(2,1)S(1)}) custom-call(bf16[2,32,4096]{2,1,0:T(8,128)(2,1)} %bitcast.18, bf16[128,512]{1,0:T(8,128)(2,1)} %bitcast.19, bf16[128,512]{1,0:T(8,128)(2,1)} %bitcast.20, bf16[2,128]{1,0:T(2,128)(2,1)} %bitcast.22, bf16[64,64]{1,0:T(8,128)(2,1)} %constant.23.clone.first_hbm, ...), custom_call_target="tpu_custom_call" | custom-call | flops 300000000 | bytes 2097152 | tf_op jit(solution)/shard_map/contrib/pallas_call | solution.py:195
  4.6 19.3 %all-to-all-start = ((bf16[64,32,128]{2,1,0:T(8,128)(2,1)}), bf16[64,32,128]{2,1,0:T(8,128)(2,1)S(1)}, u32[]{:S(2)}, u32[]{:S(2)}) async-start(bf16[64,32,128]{2,1,0:T(8,128)(2,1)} %get-tuple-element.10), calls=%async_computation | async-start | bytes 1048576 | tf_op jit(solution)/shard_map/all_to_all | solution.py:594
  23.9 2.9 %collective-permute-start = (bf16[272,512]{1,0:T(8,128)(2,1)S(1)}, bf16[272,512]{1,0:T(8,128)(2,1)S(1)}, u32[]{:S(2)}, u32[]{:S(2)}) collective-permute-start(bf16[272,512]{1,0:T(8,128)(2,1)S(1)} %get-tuple-element.11.own_ref), channel_id=1, source_target_pairs={{0,1},{1,0},{2,3},{3,2},{4,5},{5,4},{6,7},{7,6},{8,9},{9,8},{10,11... | collective-permute-start | bytes 835592 | tf_op jit(solution)/shard_map/ppermute | solution.py:595
  26.8 0.0 copy-done.3
  26.8 0.1 pad_add_fusion.sc_ref
  26.9 0.0 copy-done.2
  26.9 2.1 %slots.1.info_ref = f32[24,128]{1,0:T(8,128)S(1)} custom-call(s32[3]{0:T(128)S(1)} %pad_add_fusion.sc_ref, s32[3,8]{1,0:T(4,128)S(1)} %bitcast.17, f32[1,8,1,32]{3,2,1,0:T(1,128)S(1)} %copy-done.2, s32[2,130816]{1,0:T(2,128)} %links_ref.1, f32[256,4,512]{2,1,0:T(4,128)} %gains_ref.1), custom_call_target="tpu_custom_call" | custom-call | flops 50000000 | bytes 2097152 | tf_op jit(solution)/shard_map/slots/pallas_call | solution.py:355
  29.0 0.0 collective-permute-done.other_ref
  29.0 0.0 copy-start
  29.0 0.7 copy-done
  29.7 0.0 copy-start.1
  29.7 1.0 %copy-done.1 = bf16[272,512]{1,0:T(8,128)(2,1)S(1)} copy-done((bf16[272,512]{1,0:T(8,128)(2,1)S(1)}, bf16[272,512]{1,0:T(8,128)(2,1)}, u32[]{:S(2)}) %copy-start.1) | copy-done | bytes 278552
  30.7 4.1 %tapers.1 = (bf16[1024,1024]{1,0:T(8,128)(2,1)S(1)}, bf16[2,256,512]{2,1,0:T(8,128)(2,1)S(1)}) custom-call(s32[3]{0:T(128)S(1)} %pad_add_fusion.sc_ref, bf16[272,512]{1,0:T(8,128)(2,1)S(1)} %get-tuple-element.11.own_ref, bf16[272,512]{1,0:T(8,128)(2,1)S(1)} %copy-done.1, bf16[2,1024,512]{2,1,0:T(8,128)(2,1)} %constant.26.clone.trail_hbm, ...), custom_call_target="tpu_custom_call" | custom-call | flops 800000000 | bytes 8388608 | tf_op jit(solution)/shard_map/tapers/pallas_call | solution.py:258
  34.7 19.2 %all-to-all-done.got_ref = bf16[64,32,128]{2,1,0:T(8,128)(2,1)S(1)} async-done(((bf16[64,32,128]{2,1,0:T(8,128)(2,1)}), bf16[64,32,128]{2,1,0:T(8,128)(2,1)S(1)}, u32[]{:S(2)}, u32[]{:S(2)}) %all-to-all-start) | async-done | bytes 524320 | tf_op jit(solution)/shard_map/all_to_all | solution.py:594
  53.9 0.8 predict.1
  54.7 12.8 %all_to_all.15.got_ref = f32[8,24,128]{2,1,0:T(8,128)S(1)} all-to-all(f32[8,24,128]{2,1,0:T(8,128)S(1)} %predict.1), channel_id=1, replica_groups=mesh['facet'=64,'pol'=4,'tm'=2] {'pol','tm'}, dimensions={0} | all-to-all | bytes 196608 | tf_op jit(solution)/shard_map/all_to_all | solution.py:606
  67.6 0.2 gradient.1
  67.8 18.8 %all_to_all.16 = f32[64,1,128]{2,1,0:T(1,128)S(1)} all-to-all(f32[64,1,128]{2,1,0:T(1,128)S(1)} %bitcast.16), channel_id=1, replica_groups=mesh['facet'=64,'pol'=4,'tm'=2] {'facet'}, dimensions={0} | all-to-all | bytes 65536 | tf_op jit(solution)/shard_map/all_to_all | solution.py:608
  86.6 1.0 %collect.1 = (f32[8,128]{1,0:T(8,128)}, f32[1,8,1,32]{3,2,1,0:T(1,128)}) custom-call(f32[64,128]{1,0:T(8,128)S(1)} %bitcast.15, f32[8,32]{1,0:T(8,128)S(1)} %get-tuple-element.15.mine_ref), custom_call_target="tpu_custom_call" | custom-call | flops 2000000 | bytes 65536 | tf_op jit(solution)/shard_map/collect/pallas_call | solution.py:558
  (1 shorter events, 0.0 us)
Async XLA Ops:
  0.6 26.2 %copy-start.3 = (s32[1,1,3,8]{3,1,2,0:T(1,128)S(1)}, s32[1,1,3,8]{3,1,2,0:T(1,128)}, u32[]{:S(2)}) copy-start(s32[1,1,3,8]{3,1,2,0:T(1,128)} %param.18) | copy-start | bytes 292
  0.6 26.2 %copy-start.2 = (f32[1,8,1,32]{3,2,1,0:T(1,128)S(1)}, f32[1,8,1,32]{3,2,1,0:T(1,128)}, u32[]{:S(2)}) copy-start(f32[1,8,1,32]{3,2,1,0:T(1,128)} %obs_ref.1) | copy-start | bytes 3076
  4.6 49.3 %all-to-all-start = ((bf16[64,32,128]{2,1,0:T(8,128)(2,1)}), bf16[64,32,128]{2,1,0:T(8,128)(2,1)S(1)}, u32[]{:S(2)}, u32[]{:S(2)}) async-start(bf16[64,32,128]{2,1,0:T(8,128)(2,1)} %get-tuple-element.10), calls=%async_computation | async-start | bytes 1048576 | tf_op jit(solution)/shard_map/all_to_all | solution.py:594
  23.9 5.1 %collective-permute-start = (bf16[272,512]{1,0:T(8,128)(2,1)S(1)}, bf16[272,512]{1,0:T(8,128)(2,1)S(1)}, u32[]{:S(2)}, u32[]{:S(2)}) collective-permute-start(bf16[272,512]{1,0:T(8,128)(2,1)S(1)} %get-tuple-element.11.own_ref), channel_id=1, source_target_pairs={{0,1},{1,0},{2,3},{3,2},{4,5},{5,4},{6,7},{7,6},{8,9},{9,8},{10,11... | collective-permute-start | bytes 835592 | tf_op jit(solution)/shard_map/ppermute | solution.py:595
  29.0 0.7 copy-start
  29.7 1.0 %copy-start.1 = (bf16[272,512]{1,0:T(8,128)(2,1)S(1)}, bf16[272,512]{1,0:T(8,128)(2,1)}, u32[]{:S(2)}) copy-start(bf16[272,512]{1,0:T(8,128)(2,1)} %copy-done) | copy-start | bytes 835588

commit v5 on v4

--- a/solution.py
+++ b/solution.py
@@ -22,6 +22,7 @@
 NBLK = 8
 LINK_WINDOW = 256
 BATCHES = 2
+X_CUTS = 4
 
 w_chirp = 0.37
 grad_scale = 0.1
@@ -86,11 +87,15 @@
 ):
     rows = x_ref.shape[1]
     batch = rows // BATCHES
+    wide = FS // X_CUTS
     pieces = [
         pltpu.make_async_copy(
-            x_hbm.at[:, pl.ds(h * batch, batch), :], x_ref.at[:, pl.ds(h * batch, batch), :], x_sem.at[h]
+            x_hbm.at[:, pl.ds(h * batch, batch), pl.ds(c * wide, wide)],
+            x_ref.at[:, pl.ds(h * batch, batch), pl.ds(c * wide, wide)],
+            x_sem.at[h, c],
         )
         for h in range(BATCHES)
+        for c in range(X_CUTS)
     ]
     tables = [
         pltpu.make_async_copy(source, target, sem.at[i])
@@ -112,7 +117,7 @@
         pltpu.make_async_copy(out_ref.at[h], out_hbm.at[:, pl.ds(h * batch, batch), :], out_sem.at[h])
         for h in range(BATCHES)
     ]
-    for copy in pieces[:1] + tables + pieces[1:] + tapers:
+    for copy in pieces[:X_CUTS] + tables + pieces[X_CUTS:]:
         copy.start()
 
     def section_of(pair):
@@ -145,15 +150,19 @@
         placed[pl.ds(2 * pair + 1, 64, stride=rows), :] = result[:, 128:256]
 
     def line_up(h):
-        pieces[h].wait()
+        for c in range(X_CUTS):
+            pieces[h * X_CUTS + c].wait()
+            take(h, c)
+        for m in range(h * batch, (h + 1) * batch):
+            lined[:, m * 128 : (m + 1) * 128] = spread[pl.ds(m, 64, stride=rows), :].astype(bf16)
+
+    def take(h, c):
         for part in range(2):
-            for a in range(32):
+            for a in range(c * 32 // X_CUTS, (c + 1) * 32 // X_CUTS):
                 at = (part * 32 + a) * rows + h * batch
                 spread[at : at + batch, :] = x_ref[
                     part, h * batch : (h + 1) * batch, a * 128 : (a + 1) * 128
                 ].astype(f32)
-        for m in range(h * batch, (h + 1) * batch):
-            lined[:, m * 128 : (m + 1) * 128] = spread[pl.ds(m, 64, stride=rows), :].astype(bf16)
 
     def send(h):
         for s in range(64):
@@ -163,6 +172,8 @@
 
     per = batch // 2
     line_up(0)
+    for copy in tapers:
+        copy.start()
     for copy in tables:
         copy.wait()
     pairs = rows // 2
@@ -206,11 +217,11 @@
             pltpu.VMEM((64, 64), bf16),
             pltpu.VMEM((2, 64, 128), f32),
             pltpu.VMEM((64, 256), bf16),
-            pltpu.VMEM((64 * rows, 128), f32),
+            pltpu.VMEM((65 * rows, 128), f32),
             pltpu.VMEM((64, 128 * rows), bf16),
-            pltpu.VMEM((64 * rows, 128), f32),
+            pltpu.VMEM((65 * rows, 128), f32),
             pltpu.VMEM((BATCHES, 64, rows // BATCHES, 128), bf16),
-            pltpu.SemaphoreType.DMA((BATCHES,)),
+            pltpu.SemaphoreType.DMA((BATCHES, X_CUTS)),
             pltpu.SemaphoreType.DMA((6,)),
             pltpu.SemaphoreType.DMA((BATCHES,)),
         ],

time: 87.9 us -> 87.9 us (level)
  no operation moved by 1% of the time
where the time goes in v5:
time: 87.9 us; the launch traced here: 87.5 us
  blocking collectives  31.6 us (36%)
  starting transfers between devices  22.2 us (25%)
  waiting for transfers between devices  19.2 us (22%)
  Pallas kernels  12 us (14%)
  local copies, waits for them, and re-layouts  1.67 us (2%)
    all_to_all x1, starting transfers between devices, on_device(): lax.all_to_all(contrib, 'facet', split_axis=0, concat_axis=0, tiled=True)  19.3 us
    all_to_all x1, waiting for transfers between devices, on_device(): lax.all_to_all(contrib, 'facet', split_axis=0, concat_axis=0, tiled=True)  19.2 us
    all_to_all x1, blocking collectives, on_device(): lax.all_to_all(partial_rows.reshape(NST // 8, 1, 128), 'facet', split_axi...  18.8 us
    all_to_all x1, blocking collectives, on_device(): lax.all_to_all(sent, ('pol', 'tm'), split_axis=0, concat_axis=0, tiled=True)  12.8 us
    pallas_call x1, Pallas kernels, taper_transforms(): pl.pallas_call(taper_kernel, out_shape=(pltpu.VMEM((2 * SG, 1024), bf16),...  4.06 us
    pallas_call x1, Pallas kernels, contributions(): pl.pallas_call(contrib_kernel, out_shape=(jax.ShapeDtypeStruct((64, rows,...  3.86 us
    ppermute x1, starting transfers between devices, on_device(): other = lax.ppermute(pack, 'tm', [(0, 1), (1, 0)])  2.86 us
    pallas_call x1, Pallas kernels, slot_rows(): pl.pallas_call(slots_kernel, out_shape=jax.ShapeDtypeStruct((24, VT), f32...  2.09 us
  transfers between devices with their start and end apart: 2, of which 1 were waited for; matrix products, arithmetic and copies ran while one was open for 0% of the time, Pallas kernels for 7%

profile of v5, /device:TPU:1, one launch (start us, length us, event | category | flops | bytes accessed | tf_op | source)
XLA Modules:
  0.0 87.5 jit_solution(3640793070322602165)
XLA Ops:
  0.6 0.0 copy-start.3
  0.6 0.0 copy-start.2
  0.7 3.9 %contrib.1 = (bf16[64,32,128]{2,1,0:T(8,128)(2,1)}, bf16[272,512]{1,0:T(8,128)(2,1)S(1)}) custom-call(bf16[2,32,4096]{2,1,0:T(8,128)(2,1)} %bitcast.18, bf16[128,512]{1,0:T(8,128)(2,1)} %bitcast.19, bf16[128,512]{1,0:T(8,128)(2,1)} %bitcast.20, bf16[2,128]{1,0:T(2,128)(2,1)} %bitcast.22, bf16[64,64]{1,0:T(8,128)(2,1)} %constant.23.clone.first_hbm, ...), custom_call_target="tpu_custom_call" | custom-call | flops 300000000 | bytes 2097152 | tf_op jit(solution)/shard_map/contrib/pallas_call | solution.py:206
  4.5 19.3 %all-to-all-start = ((bf16[64,32,128]{2,1,0:T(8,128)(2,1)}), bf16[64,32,128]{2,1,0:T(8,128)(2,1)S(1)}, u32[]{:S(2)}, u32[]{:S(2)}) async-start(bf16[64,32,128]{2,1,0:T(8,128)(2,1)} %get-tuple-element.10), calls=%async_computation | async-start | bytes 1048576 | tf_op jit(solution)/shard_map/all_to_all | solution.py:605
  23.8 2.9 %collective-permute-start = (bf16[272,512]{1,0:T(8,128)(2,1)S(1)}, bf16[272,512]{1,0:T(8,128)(2,1)S(1)}, u32[]{:S(2)}, u32[]{:S(2)}) collective-permute-start(bf16[272,512]{1,0:T(8,128)(2,1)S(1)} %get-tuple-element.11.own_ref), channel_id=1, source_target_pairs={{0,1},{1,0},{2,3},{3,2},{4,5},{5,4},{6,7},{7,6},{8,9},{9,8},{10,11... | collective-permute-start | bytes 835592 | tf_op jit(solution)/shard_map/ppermute | solution.py:606
  26.7 0.0 copy-done.3
  26.7 0.1 pad_add_fusion.sc_ref
  26.8 0.0 copy-done.2
  26.8 2.1 %slots.1.info_ref = f32[24,128]{1,0:T(8,128)S(1)} custom-call(s32[3]{0:T(128)S(1)} %pad_add_fusion.sc_ref, s32[3,8]{1,0:T(4,128)S(1)} %bitcast.17, f32[1,8,1,32]{3,2,1,0:T(1,128)S(1)} %copy-done.2, s32[2,130816]{1,0:T(2,128)} %links_ref.1, f32[256,4,512]{2,1,0:T(4,128)} %gains_ref.1), custom_call_target="tpu_custom_call" | custom-call | flops 50000000 | bytes 2097152 | tf_op jit(solution)/shard_map/slots/pallas_call | solution.py:366
  28.9 0.0 collective-permute-done.other_ref
  28.9 0.0 copy-start
  28.9 0.7 copy-done
  29.6 0.0 copy-start.1
  29.6 1.0 %copy-done.1 = bf16[272,512]{1,0:T(8,128)(2,1)S(1)} copy-done((bf16[272,512]{1,0:T(8,128)(2,1)S(1)}, bf16[272,512]{1,0:T(8,128)(2,1)}, u32[]{:S(2)}) %copy-start.1) | copy-done | bytes 278552
  30.6 4.1 %tapers.1 = (bf16[1024,1024]{1,0:T(8,128)(2,1)S(1)}, bf16[2,256,512]{2,1,0:T(8,128)(2,1)S(1)}) custom-call(s32[3]{0:T(128)S(1)} %pad_add_fusion.sc_ref, bf16[272,512]{1,0:T(8,128)(2,1)S(1)} %get-tuple-element.11.own_ref, bf16[272,512]{1,0:T(8,128)(2,1)S(1)} %copy-done.1, bf16[2,1024,512]{2,1,0:T(8,128)(2,1)} %constant.26.clone.trail_hbm, ...), custom_call_target="tpu_custom_call" | custom-call | flops 800000000 | bytes 8388608 | tf_op jit(solution)/shard_map/tapers/pallas_call | solution.py:269
  34.6 19.2 %all-to-all-done.got_ref = bf16[64,32,128]{2,1,0:T(8,128)(2,1)S(1)} async-done(((bf16[64,32,128]{2,1,0:T(8,128)(2,1)}), bf16[64,32,128]{2,1,0:T(8,128)(2,1)S(1)}, u32[]{:S(2)}, u32[]{:S(2)}) %all-to-all-start) | async-done | bytes 524320 | tf_op jit(solution)/shard_map/all_to_all | solution.py:605
  53.8 0.8 predict.1
  54.6 12.8 %all_to_all.15.got_ref = f32[8,24,128]{2,1,0:T(8,128)S(1)} all-to-all(f32[8,24,128]{2,1,0:T(8,128)S(1)} %predict.1), channel_id=1, replica_groups=mesh['facet'=64,'pol'=4,'tm'=2] {'pol','tm'}, dimensions={0} | all-to-all | bytes 196608 | tf_op jit(solution)/shard_map/all_to_all | solution.py:617
  67.5 0.2 gradient.1
  67.7 18.8 %all_to_all.16 = f32[64,1,128]{2,1,0:T(1,128)S(1)} all-to-all(f32[64,1,128]{2,1,0:T(1,128)S(1)} %bitcast.16), channel_id=1, replica_groups=mesh['facet'=64,'pol'=4,'tm'=2] {'facet'}, dimensions={0} | all-to-all | bytes 65536 | tf_op jit(solution)/shard_map/all_to_all | solution.py:619
  86.5 1.0 %collect.1 = (f32[8,128]{1,0:T(8,128)}, f32[1,8,1,32]{3,2,1,0:T(1,128)}) custom-call(f32[64,128]{1,0:T(8,128)S(1)} %bitcast.15, f32[8,32]{1,0:T(8,128)S(1)} %get-tuple-element.15.mine_ref), custom_call_target="tpu_custom_call" | custom-call | flops 2000000 | bytes 65536 | tf_op jit(solution)/shard_map/collect/pallas_call | solution.py:569
  (1 shorter events, 0.0 us)
Async XLA Ops:
  0.6 26.1 %copy-start.3 = (s32[1,1,3,8]{3,1,2,0:T(1,128)S(1)}, s32[1,1,3,8]{3,1,2,0:T(1,128)}, u32[]{:S(2)}) copy-start(s32[1,1,3,8]{3,1,2,0:T(1,128)} %param.18) | copy-start | bytes 292
  0.6 26.2 %copy-start.2 = (f32[1,8,1,32]{3,2,1,0:T(1,128)S(1)}, f32[1,8,1,32]{3,2,1,0:T(1,128)}, u32[]{:S(2)}) copy-start(f32[1,8,1,32]{3,2,1,0:T(1,128)} %obs_ref.1) | copy-start | bytes 3076
  4.5 49.3 %all-to-all-start = ((bf16[64,32,128]{2,1,0:T(8,128)(2,1)}), bf16[64,32,128]{2,1,0:T(8,128)(2,1)S(1)}, u32[]{:S(2)}, u32[]{:S(2)}) async-start(bf16[64,32,128]{2,1,0:T(8,128)(2,1)} %get-tuple-element.10), calls=%async_computation | async-start | bytes 1048576 | tf_op jit(solution)/shard_map/all_to_all | solution.py:605
  23.8 5.1 %collective-permute-start = (bf16[272,512]{1,0:T(8,128)(2,1)S(1)}, bf16[272,512]{1,0:T(8,128)(2,1)S(1)}, u32[]{:S(2)}, u32[]{:S(2)}) collective-permute-start(bf16[272,512]{1,0:T(8,128)(2,1)S(1)} %get-tuple-element.11.own_ref), channel_id=1, source_target_pairs={{0,1},{1,0},{2,3},{3,2},{4,5},{5,4},{6,7},{7,6},{8,9},{9,8},{10,11... | collective-permute-start | bytes 835592 | tf_op jit(solution)/shard_map/ppermute | solution.py:606
  28.9 0.7 copy-start
  29.6 1.0 %copy-start.1 = (bf16[272,512]{1,0:T(8,128)(2,1)S(1)}, bf16[272,512]{1,0:T(8,128)(2,1)}, u32[]{:S(2)}) copy-start(bf16[272,512]{1,0:T(8,128)(2,1)} %copy-done) | copy-start | bytes 835588

commit v6 on v5

--- a/solution.py
+++ b/solution.py
@@ -536,20 +536,16 @@
 
 
 def collect_kernel(got_ref, mine_ref, out_hbm, resid_hbm, out_ref, resid_ref, sem):
-    part = mine_ref[...]
-    for row in range(2 * NPOL):
-        resid_ref[0, row] = part[row : row + 1, :]
-    resid_copy = pltpu.make_async_copy(resid_ref, resid_hbm, sem.at[0])
-    resid_copy.start()
     turned = got_ref[...].T
-    lanes = turned.shape[1]
+    lanes = 2 * turned.shape[1]
     channel_row = lax.broadcasted_iota(jnp.int32, (128, lanes), 0) >> 2
     group_row = lax.broadcasted_iota(jnp.int32, (8, lanes), 0)
     values = []
     groups = []
-    for block in range(2 * NBLK):
-        channel = turned[64 + block : 65 + block].astype(jnp.int32)
-        terms = turned[4 * block : 4 * block + 4]
+    for block in range(NBLK):
+        pair = (block, block + NBLK)
+        channel = jnp.concatenate([turned[64 + b : 65 + b] for b in pair], axis=1).astype(jnp.int32)
+        terms = jnp.concatenate([turned[4 * b : 4 * b + 4] for b in pair], axis=1)
         tall = jnp.concatenate([terms, terms], axis=0)
         tall = jnp.concatenate([tall] * 16, axis=0)
         value = jnp.where(channel_row == (channel & 31), tall, 0.0).astype(bf16)
@@ -560,6 +556,11 @@
     out_ref[...] = grad_scale * total
     out_copy = pltpu.make_async_copy(out_ref, out_hbm, sem.at[1])
     out_copy.start()
+    part = mine_ref[...]
+    for row in range(2 * NPOL):
+        resid_ref[0, row] = part[row : row + 1, :]
+    resid_copy = pltpu.make_async_copy(resid_ref, resid_hbm, sem.at[0])
+    resid_copy.start()
     out_copy.wait()
     resid_copy.wait()
 

time: 87.9 us -> 87.9 us (level)
  no operation moved by 1% of the time
where the time goes in v6:
time: 87.9 us; the launch traced here: 87.5 us
  blocking collectives  31.6 us (36%)
  starting transfers between devices  22.2 us (25%)
  waiting for transfers between devices  19.2 us (22%)
  Pallas kernels  12 us (14%)
  local copies, waits for them, and re-layouts  1.67 us (2%)
    all_to_all x1, starting transfers between devices, on_device(): lax.all_to_all(contrib, 'facet', split_axis=0, concat_axis=0, tiled=True)  19.3 us
    all_to_all x1, waiting for transfers between devices, on_device(): lax.all_to_all(contrib, 'facet', split_axis=0, concat_axis=0, tiled=True)  19.2 us
    all_to_all x1, blocking collectives, on_device(): lax.all_to_all(partial_rows.reshape(NST // 8, 1, 128), 'facet', split_axi...  18.8 us
    all_to_all x1, blocking collectives, on_device(): lax.all_to_all(sent, ('pol', 'tm'), split_axis=0, concat_axis=0, tiled=True)  12.8 us
    pallas_call x1, Pallas kernels, taper_transforms(): pl.pallas_call(taper_kernel, out_shape=(pltpu.VMEM((2 * SG, 1024), bf16),...  4.06 us
    pallas_call x1, Pallas kernels, contributions(): pl.pallas_call(contrib_kernel, out_shape=(jax.ShapeDtypeStruct((64, rows,...  3.86 us
    ppermute x1, starting transfers between devices, on_device(): other = lax.ppermute(pack, 'tm', [(0, 1), (1, 0)])  2.86 us
    pallas_call x1, Pallas kernels, slot_rows(): pl.pallas_call(slots_kernel, out_shape=jax.ShapeDtypeStruct((24, VT), f32...  2.09 us
  transfers between devices with their start and end apart: 2, of which 1 were waited for; matrix products, arithmetic and copies ran while one was open for 0% of the time, Pallas kernels for 7%

profile of v6, /device:TPU:1, one launch (start us, length us, event | category | flops | bytes accessed | tf_op | source)
XLA Modules:
  0.0 87.5 jit_solution(8571153542080601264)
XLA Ops:
  0.6 0.0 copy-start.3
  0.6 0.0 copy-start.2
  0.7 3.9 %contrib.1 = (bf16[64,32,128]{2,1,0:T(8,128)(2,1)}, bf16[272,512]{1,0:T(8,128)(2,1)S(1)}) custom-call(bf16[2,32,4096]{2,1,0:T(8,128)(2,1)} %bitcast.18, bf16[128,512]{1,0:T(8,128)(2,1)} %bitcast.19, bf16[128,512]{1,0:T(8,128)(2,1)} %bitcast.20, bf16[2,128]{1,0:T(2,128)(2,1)} %bitcast.22, bf16[64,64]{1,0:T(8,128)(2,1)} %constant.23.clone.first_hbm, ...), custom_call_target="tpu_custom_call" | custom-call | flops 300000000 | bytes 2097152 | tf_op jit(solution)/shard_map/contrib/pallas_call | solution.py:206
  4.5 19.3 %all-to-all-start = ((bf16[64,32,128]{2,1,0:T(8,128)(2,1)}), bf16[64,32,128]{2,1,0:T(8,128)(2,1)S(1)}, u32[]{:S(2)}, u32[]{:S(2)}) async-start(bf16[64,32,128]{2,1,0:T(8,128)(2,1)} %get-tuple-element.10), calls=%async_computation | async-start | bytes 1048576 | tf_op jit(solution)/shard_map/all_to_all | solution.py:606
  23.8 2.9 %collective-permute-start = (bf16[272,512]{1,0:T(8,128)(2,1)S(1)}, bf16[272,512]{1,0:T(8,128)(2,1)S(1)}, u32[]{:S(2)}, u32[]{:S(2)}) collective-permute-start(bf16[272,512]{1,0:T(8,128)(2,1)S(1)} %get-tuple-element.11.own_ref), channel_id=1, source_target_pairs={{0,1},{1,0},{2,3},{3,2},{4,5},{5,4},{6,7},{7,6},{8,9},{9,8},{10,11... | collective-permute-start | bytes 835592 | tf_op jit(solution)/shard_map/ppermute | solution.py:607
  26.7 0.0 copy-done.3
  26.7 0.1 pad_add_fusion.sc_ref
  26.8 0.0 copy-done.2
  26.8 2.1 %slots.1.info_ref = f32[24,128]{1,0:T(8,128)S(1)} custom-call(s32[3]{0:T(128)S(1)} %pad_add_fusion.sc_ref, s32[3,8]{1,0:T(4,128)S(1)} %bitcast.17, f32[1,8,1,32]{3,2,1,0:T(1,128)S(1)} %copy-done.2, s32[2,130816]{1,0:T(2,128)} %links_ref.1, f32[256,4,512]{2,1,0:T(4,128)} %gains_ref.1), custom_call_target="tpu_custom_call" | custom-call | flops 50000000 | bytes 2097152 | tf_op jit(solution)/shard_map/slots/pallas_call | solution.py:366
  28.9 0.0 collective-permute-done.other_ref
  28.9 0.0 copy-start
  28.9 0.7 copy-done
  29.6 0.0 copy-start.1
  29.6 1.0 %copy-done.1 = bf16[272,512]{1,0:T(8,128)(2,1)S(1)} copy-done((bf16[272,512]{1,0:T(8,128)(2,1)S(1)}, bf16[272,512]{1,0:T(8,128)(2,1)}, u32[]{:S(2)}) %copy-start.1) | copy-done | bytes 278552
  30.6 4.1 %tapers.1 = (bf16[1024,1024]{1,0:T(8,128)(2,1)S(1)}, bf16[2,256,512]{2,1,0:T(8,128)(2,1)S(1)}) custom-call(s32[3]{0:T(128)S(1)} %pad_add_fusion.sc_ref, bf16[272,512]{1,0:T(8,128)(2,1)S(1)} %get-tuple-element.11.own_ref, bf16[272,512]{1,0:T(8,128)(2,1)S(1)} %copy-done.1, bf16[2,1024,512]{2,1,0:T(8,128)(2,1)} %constant.26.clone.trail_hbm, ...), custom_call_target="tpu_custom_call" | custom-call | flops 800000000 | bytes 8388608 | tf_op jit(solution)/shard_map/tapers/pallas_call | solution.py:269
  34.6 19.2 %all-to-all-done.got_ref = bf16[64,32,128]{2,1,0:T(8,128)(2,1)S(1)} async-done(((bf16[64,32,128]{2,1,0:T(8,128)(2,1)}), bf16[64,32,128]{2,1,0:T(8,128)(2,1)S(1)}, u32[]{:S(2)}, u32[]{:S(2)}) %all-to-all-start) | async-done | bytes 524320 | tf_op jit(solution)/shard_map/all_to_all | solution.py:606
  53.8 0.8 predict.1
  54.6 12.8 %all_to_all.15.got_ref = f32[8,24,128]{2,1,0:T(8,128)S(1)} all-to-all(f32[8,24,128]{2,1,0:T(8,128)S(1)} %predict.1), channel_id=1, replica_groups=mesh['facet'=64,'pol'=4,'tm'=2] {'pol','tm'}, dimensions={0} | all-to-all | bytes 196608 | tf_op jit(solution)/shard_map/all_to_all | solution.py:618
  67.5 0.2 gradient.1
  67.7 18.8 %all_to_all.16 = f32[64,1,128]{2,1,0:T(1,128)S(1)} all-to-all(f32[64,1,128]{2,1,0:T(1,128)S(1)} %bitcast.16), channel_id=1, replica_groups=mesh['facet'=64,'pol'=4,'tm'=2] {'facet'}, dimensions={0} | all-to-all | bytes 65536 | tf_op jit(solution)/shard_map/all_to_all | solution.py:620
  86.5 1.0 %collect.1 = (f32[8,128]{1,0:T(8,128)}, f32[1,8,1,32]{3,2,1,0:T(1,128)}) custom-call(f32[64,128]{1,0:T(8,128)S(1)} %bitcast.15, f32[8,32]{1,0:T(8,128)S(1)} %get-tuple-element.15.mine_ref), custom_call_target="tpu_custom_call" | custom-call | flops 2000000 | bytes 65536 | tf_op jit(solution)/shard_map/collect/pallas_call | solution.py:570
  (1 shorter events, 0.0 us)
Async XLA Ops:
  0.6 26.1 %copy-start.3 = (s32[1,1,3,8]{3,1,2,0:T(1,128)S(1)}, s32[1,1,3,8]{3,1,2,0:T(1,128)}, u32[]{:S(2)}) copy-start(s32[1,1,3,8]{3,1,2,0:T(1,128)} %param.18) | copy-start | bytes 292
  0.6 26.2 %copy-start.2 = (f32[1,8,1,32]{3,2,1,0:T(1,128)S(1)}, f32[1,8,1,32]{3,2,1,0:T(1,128)}, u32[]{:S(2)}) copy-start(f32[1,8,1,32]{3,2,1,0:T(1,128)} %obs_ref.1) | copy-start | bytes 3076
  4.5 49.3 %all-to-all-start = ((bf16[64,32,128]{2,1,0:T(8,128)(2,1)}), bf16[64,32,128]{2,1,0:T(8,128)(2,1)S(1)}, u32[]{:S(2)}, u32[]{:S(2)}) async-start(bf16[64,32,128]{2,1,0:T(8,128)(2,1)} %get-tuple-element.10), calls=%async_computation | async-start | bytes 1048576 | tf_op jit(solution)/shard_map/all_to_all | solution.py:606
  23.8 5.1 %collective-permute-start = (bf16[272,512]{1,0:T(8,128)(2,1)S(1)}, bf16[272,512]{1,0:T(8,128)(2,1)S(1)}, u32[]{:S(2)}, u32[]{:S(2)}) collective-permute-start(bf16[272,512]{1,0:T(8,128)(2,1)S(1)} %get-tuple-element.11.own_ref), channel_id=1, source_target_pairs={{0,1},{1,0},{2,3},{3,2},{4,5},{5,4},{6,7},{7,6},{8,9},{9,8},{10,11... | collective-permute-start | bytes 835592 | tf_op jit(solution)/shard_map/ppermute | solution.py:607
  28.9 0.7 copy-start
  29.6 1.0 %copy-start.1 = (bf16[272,512]{1,0:T(8,128)(2,1)S(1)}, bf16[272,512]{1,0:T(8,128)(2,1)}, u32[]{:S(2)}) copy-start(bf16[272,512]{1,0:T(8,128)(2,1)} %copy-done) | copy-start | bytes 835588
